TPU v7x, 128 devices: a whole 4x4x4 slice. The times are simulated.
128 devices in a mesh: grp: 4 (over x), dev: 32 (over y, z, core).
Axes of the slice: x: 4, y: 4, z: 4, core: 2. Of those that a mesh axis runs over, the one named last changes fastest.
Arguments:
- positions: bfloat16 [3, 524288], P(None, ('grp', 'dev')), may hold values from 0 to 1.5
- features: bfloat16 [524288, 128], P(('grp', 'dev')), may hold values from -6 to 6
- tile_first: int32 [1024], P(('grp', 'dev')), may hold values from 0 to 31
- tile_second: int32 [1024], P(('grp', 'dev')), may hold values from 0 to 127
- count_first: int32 [1024], P(('grp', 'dev')), may hold values from 32 to 128
- count_second: int32 [1024], P(('grp', 'dev')), may hold values from 32 to 128
- w_first: bfloat16 [128, 128], replicated, may hold values from -0.5 to 0.5
- w_second: bfloat16 [128, 128], replicated, may hold values from -0.5 to 0.5
- radial_weight: bfloat16 [16, 128], replicated, may hold values from -3 to 3
- mix_weight: bfloat16 [128, 128], replicated, may hold values from -0.5 to 0.5
- out_weight: float32 [128], replicated, may hold values from -1.5 to 1.5
Outputs:
- forces: float32 [3, 524288], P(None, ('grp', 'dev'))
All inputs are finite; a program needn't handle non-finite values.
Results may differ from a plain program's by a relative error of at most 0.0023.
Values may be sent and summed in bfloat16 or wider, within the bound.
A program may use at most 64 MiB of HBM per device.

v0:
```python
import jax
import jax.numpy as jnp
from jax import lax
from jax.sharding import PartitionSpec as P

CELL = 128
NB = 16


def passed_along(array, axis, by):
    count = lax.axis_size(axis)
    return lax.ppermute(array, axis, [(i, (i + by) % count) for i in range(count)])


def project(features, weight):
    return jnp.dot(features, weight, preferred_element_type=jnp.float32).astype(jnp.bfloat16)


def silu_slope(values):
    sigma = jax.nn.sigmoid(values)
    return sigma * (1.0 + values * (1.0 - sigma))


def tile_gradients(
    first_pos,
    second_pos,
    first_proj,
    second_proj,
    first_live,
    second_live,
    radial_weight,
    mix_weight,
    out_weight,
):
    slots = first_pos.shape[1]
    diff = first_pos[:, :, None] - second_pos[:, None, :]
    dist_sq = jnp.sum(diff * diff, axis=0).reshape(-1)
    centers = jnp.arange(NB, dtype=jnp.float32) * (6.75 / NB)
    offset = dist_sq[None, :] - centers[:, None]
    basis_exact = jnp.exp(-2.0 * offset * offset)
    basis = basis_exact.astype(jnp.bfloat16)
    radial = lax.dot_general(
        basis, radial_weight, (((0,), (0,)), ((), ())), preferred_element_type=jnp.float32
    )
    radial = radial.reshape(slots, slots, -1)
    summed = (
        radial
        + first_proj.astype(jnp.float32)[:, None, :]
        + second_proj.astype(jnp.float32)[None, :, :]
    )
    summed = summed.reshape(slots * slots, -1)
    latent = jax.nn.silu(summed).astype(jnp.bfloat16)
    pre = jnp.dot(latent, mix_weight, preferred_element_type=jnp.float32)
    readout = jnp.sum(jax.nn.silu(pre) * out_weight[None, :], axis=1)
    weights = (first_live[:, None] * second_live[None, :]).reshape(-1) / slots
    envelope_base = 1.0 - dist_sq / 8.0
    envelope = envelope_base * envelope_base
    d_readout = envelope * weights
    d_pre = (d_readout[:, None] * out_weight[None, :] * silu_slope(pre)).astype(jnp.bfloat16)
    d_latent = lax.dot_general(
        d_pre, mix_weight, (((1,), (1,)), ((), ())), preferred_element_type=jnp.float32
    )
    d_summed = (d_latent * silu_slope(summed)).astype(jnp.bfloat16)
    d_basis = lax.dot_general(
        radial_weight, d_summed, (((1,), (1,)), ((), ())), preferred_element_type=jnp.float32
    )
    d_dist = jnp.sum(d_basis * basis_exact * (-4.0 * offset), axis=0)
    d_dist = d_dist + readout * weights * 2.0 * envelope_base * -0.125
    d_dist = d_dist.reshape(slots, slots)
    pull = 2.0 * diff * d_dist[None, :, :]
    return (jnp.sum(pull, axis=2), -jnp.sum(pull, axis=1))


def live_mask(count):
    return (jnp.arange(CELL, dtype=jnp.int32) < count).astype(jnp.float32)


def on_device(
    positions,
    features,
    tile_first,
    tile_second,
    count_first,
    count_second,
    w_first,
    w_second,
    radial_weight,
    mix_weight,
    out_weight,
):
    slot_count = positions.shape[1]
    beside = passed_along((positions, features), "dev", 1)
    upper = passed_along((positions, features, beside[0], beside[1]), "grp", 1)
    area_pos = jnp.concatenate([positions, beside[0], upper[0], upper[2]], axis=1).astype(
        jnp.float32
    )
    area_sent = jnp.concatenate([features, beside[1], upper[1], upper[3]], axis=0)
    area_second = project(area_sent, w_second)
    own_first = project(features, w_first)

    def visit(index, total):
        start_a = tile_first[index] * CELL
        start_b = tile_second[index] * CELL
        pos_a = lax.dynamic_slice_in_dim(area_pos, start_a, CELL, 1)
        pos_b = lax.dynamic_slice_in_dim(area_pos, start_b, CELL, 1)
        proj_a = lax.dynamic_slice_in_dim(own_first, start_a, CELL, 0)
        proj_b = lax.dynamic_slice_in_dim(area_second, start_b, CELL, 0)
        grad_a, grad_b = tile_gradients(
            pos_a,
            pos_b,
            proj_a,
            proj_b,
            live_mask(count_first[index]),
            live_mask(count_second[index]),
            radial_weight,
            mix_weight,
            out_weight,
        )
        total = lax.dynamic_update_slice_in_dim(
            total, lax.dynamic_slice_in_dim(total, start_a, CELL, 1) + grad_a, start_a, 1
        )
        total = lax.dynamic_update_slice_in_dim(
            total, lax.dynamic_slice_in_dim(total, start_b, CELL, 1) + grad_b, start_b, 1
        )
        return total

    total = lax.fori_loop(
        0, tile_first.shape[0], visit, jnp.zeros((3, 4 * slot_count), jnp.float32)
    )
    own_part = total[:, :slot_count]
    beside_part = total[:, slot_count : 2 * slot_count]
    upper_part = total[:, 2 * slot_count : 3 * slot_count]
    corner_part = total[:, 3 * slot_count :]
    received = passed_along((beside_part, corner_part), "dev", -1)
    lifted = passed_along(upper_part + received[1], "grp", -1)
    gradient = own_part + received[0] + lifted
    return -gradient


def solution(mesh):
    in_specs = (
        P(None, ("grp", "dev")),
        P(("grp", "dev"), None),
        P(("grp", "dev")),
        P(("grp", "dev")),
        P(("grp", "dev")),
        P(("grp", "dev")),
        P(),
        P(),
        P(),
        P(),
        P(),
    )
    out_specs = P(None, ("grp", "dev"))
    return jax.shard_map(
        on_device, mesh=mesh, in_specs=in_specs, out_specs=out_specs, check_vma=False
    )
```

profile of v0, /device:TPU:0, one launch (start us, length us, event | category | flops | bytes accessed | tf_op | source)
XLA Modules:
  0.0 281.0 jit_solution(13357502688930973997)
XLA Ops:
  0.0 2.1 collective-permute-start
  2.1 1.5 collective-permute-start.4
  3.6 1.5 collective-permute-start.1
  5.1 14.0 %collective-permute-done = bf16[3,4096]{1,0:T(4,128)(2,1)S(1)} collective-permute-done((bf16[3,4096]{1,0:T(4,128)(2,1)}, bf16[3,4096]{1,0:T(4,128)(2,1)S(1)}, u32[]{:S(2)}, u32[]{:S(2)}) %collective-permute-start) | collective-permute-done | bytes 24608 | tf_op jit(solution)/shard_map/ppermute | solution.py:12
  19.1 1.5 collective-permute-start.2
  20.5 1.6 convolution_convert_fusion.1
  22.2 1.7 collective-permute-start.5
  23.9 6.3 %collective-permute-done.1 = bf16[3,4096]{1,0:T(4,128)(2,1)S(1)} collective-permute-done((bf16[3,4096]{1,0:T(4,128)(2,1)}, bf16[3,4096]{1,0:T(4,128)(2,1)S(1)}, u32[]{:S(2)}, u32[]{:S(2)}) %collective-permute-start.1) | collective-permute-done | bytes 24608 | tf_op jit(solution)/shard_map/ppermute | solution.py:12
  31.9 20.7 %collective-permute-done.5 = bf16[4096,128]{1,0:T(8,128)(2,1)S(1)} collective-permute-done((bf16[4096,128]{1,0:T(8,128)(2,1)S(1)}, bf16[4096,128]{1,0:T(8,128)(2,1)S(1)}, u32[]{:S(2)}, u32[]{:S(2)}) %collective-permute-start.5) | collective-permute-done | bytes 1048608 | tf_op jit(solution)/shard_map/ppermute | solution.py:12
  52.6 4.8 %convolution_convert_fusion = bf16[16384,128]{1,0:T(8,128)(2,1)} fusion(bf16[128,128]{1,0:T(8,128)(2,1)S(1)} %copy-done, bf16[4096,128]{1,0:T(8,128)(2,1)S(1)} %collective-permute-done.5, bf16[4096,128]{1,0:T(8,128)(2,1)} %collective-permute-done.4, bf16[4096,128]{1,0:T(8,128)(2,1)S(1)} %collective-permute-done.3, bf16[4096,128]{1,0:T(8,128)(2,1)} %param.14), kind=kOutput, calls=%fused_computation.50 | convolution fusion | flops 555745280 | bytes 8421376 | tf_op jit(solution)/shard_map/dot_general | solution.py:16
  57.5 213.6 %while.13 = (s32[]{:T(128)}, f32[3,16384]{1,0:T(4,128)S(1)}, s32[8]{0:T(128)S(1)}, f32[3,16384]{1,0:T(4,128)S(1)}, s32[8]{0:T(128)S(1)}, /*index=5*/s32[8]{0:T(1...) while((s32[]{:T(128)}, f32[3,16384]{1,0:T(4,128)S(1)}, ...), condition=%wide.region_6.7_spmd, body=%wide.region_0.6_spmd.sunk | while | flops 1278542720 | bytes 110337600 | solution.py:127
  62.5 1.4 fusion.59
  64.0 7.0 %multiply_reduce_fusion.2 = (f32[16384]{0:T(1024)S(1)}, f32[16384,128]{1,0:T(8,128)}) fusion(f32[128]{0:T(128)S(1)} %get-tuple-element.375, bf16[128,128]{1,0:T(8,128)(2,1)S(1)} %get-tuple-element.379, f32[16384,128]{1,0:T(8,128)S(1)} %fusion.59), kind=kOutput, calls=%fused_computation.7.clone.1 | convolution fusion | flops 559923200 | bytes 16876032 | tf_op jit(solution)/shard_map/while/body/eval_jaxpr/dot_general | solution.py:53
  72.2 1.3 compare_convert_fusion.3
  73.5 10.2 %fusion.60 = f32[16384]{0:T(1024)S(1)} fusion(bf16[16,128]{1,0:T(8,128)(2,1)S(1)} %get-tuple-element.376, bf16[128,128]{1,0:T(8,128)(2,1)S(1)} %get-tuple-element.379, f32[16384,128]{1,0:T(8,128)} %copy-done.1, f32[16384,128]{1,0:T(8,128)} %get-tuple-element.329, f32[128]{0:T(128)S(1)} %get-tuple-element.375, f32[16384]{0:T(1024)S(1)} %bitcast_multiply_fusion.3, ...), kind=kOutput, calls=%fused_computation.19.clone.1 | convolution fusion | flops 645644288 | bytes 17011264 | tf_op jit(solution)/shard_map/while/body/eval_jaxpr/dot_general | solution.py:64
  89.2 1.4 fusion.59
  90.7 7.0 %multiply_reduce_fusion.2 = (f32[16384]{0:T(1024)S(1)}, f32[16384,128]{1,0:T(8,128)}) fusion(f32[128]{0:T(128)S(1)} %get-tuple-element.375, bf16[128,128]{1,0:T(8,128)(2,1)S(1)} %get-tuple-element.379, f32[16384,128]{1,0:T(8,128)S(1)} %fusion.59), kind=kOutput, calls=%fused_computation.7.clone.1 | convolution fusion | flops 559923200 | bytes 16876032 | tf_op jit(solution)/shard_map/while/body/eval_jaxpr/dot_general | solution.py:53
  98.9 1.3 compare_convert_fusion.3
  100.2 10.2 %fusion.60 = f32[16384]{0:T(1024)S(1)} fusion(bf16[16,128]{1,0:T(8,128)(2,1)S(1)} %get-tuple-element.376, bf16[128,128]{1,0:T(8,128)(2,1)S(1)} %get-tuple-element.379, f32[16384,128]{1,0:T(8,128)} %copy-done.1, f32[16384,128]{1,0:T(8,128)} %get-tuple-element.329, f32[128]{0:T(128)S(1)} %get-tuple-element.375, f32[16384]{0:T(1024)S(1)} %bitcast_multiply_fusion.3, ...), kind=kOutput, calls=%fused_computation.19.clone.1 | convolution fusion | flops 645644288 | bytes 17011264 | tf_op jit(solution)/shard_map/while/body/eval_jaxpr/dot_general | solution.py:64
  115.9 1.4 fusion.59
  117.4 7.0 %multiply_reduce_fusion.2 = (f32[16384]{0:T(1024)S(1)}, f32[16384,128]{1,0:T(8,128)}) fusion(f32[128]{0:T(128)S(1)} %get-tuple-element.375, bf16[128,128]{1,0:T(8,128)(2,1)S(1)} %get-tuple-element.379, f32[16384,128]{1,0:T(8,128)S(1)} %fusion.59), kind=kOutput, calls=%fused_computation.7.clone.1 | convolution fusion | flops 559923200 | bytes 16876032 | tf_op jit(solution)/shard_map/while/body/eval_jaxpr/dot_general | solution.py:53
  125.6 1.3 compare_convert_fusion.3
  126.9 10.2 %fusion.60 = f32[16384]{0:T(1024)S(1)} fusion(bf16[16,128]{1,0:T(8,128)(2,1)S(1)} %get-tuple-element.376, bf16[128,128]{1,0:T(8,128)(2,1)S(1)} %get-tuple-element.379, f32[16384,128]{1,0:T(8,128)} %copy-done.1, f32[16384,128]{1,0:T(8,128)} %get-tuple-element.329, f32[128]{0:T(128)S(1)} %get-tuple-element.375, f32[16384]{0:T(1024)S(1)} %bitcast_multiply_fusion.3, ...), kind=kOutput, calls=%fused_computation.19.clone.1 | convolution fusion | flops 645644288 | bytes 17011264 | tf_op jit(solution)/shard_map/while/body/eval_jaxpr/dot_general | solution.py:64
  141.0 1.0 add.237
  142.6 1.4 fusion.59
  144.1 7.0 %multiply_reduce_fusion.2 = (f32[16384]{0:T(1024)S(1)}, f32[16384,128]{1,0:T(8,128)}) fusion(f32[128]{0:T(128)S(1)} %get-tuple-element.375, bf16[128,128]{1,0:T(8,128)(2,1)S(1)} %get-tuple-element.379, f32[16384,128]{1,0:T(8,128)S(1)} %fusion.59), kind=kOutput, calls=%fused_computation.7.clone.1 | convolution fusion | flops 559923200 | bytes 16876032 | tf_op jit(solution)/shard_map/while/body/eval_jaxpr/dot_general | solution.py:53
  152.3 1.3 compare_convert_fusion.3
  153.6 10.2 %fusion.60 = f32[16384]{0:T(1024)S(1)} fusion(bf16[16,128]{1,0:T(8,128)(2,1)S(1)} %get-tuple-element.376, bf16[128,128]{1,0:T(8,128)(2,1)S(1)} %get-tuple-element.379, f32[16384,128]{1,0:T(8,128)} %copy-done.1, f32[16384,128]{1,0:T(8,128)} %get-tuple-element.329, f32[128]{0:T(128)S(1)} %get-tuple-element.375, f32[16384]{0:T(1024)S(1)} %bitcast_multiply_fusion.3, ...), kind=kOutput, calls=%fused_computation.19.clone.1 | convolution fusion | flops 645644288 | bytes 17011264 | tf_op jit(solution)/shard_map/while/body/eval_jaxpr/dot_general | solution.py:64
  169.3 1.4 fusion.59
  170.8 7.0 %multiply_reduce_fusion.2 = (f32[16384]{0:T(1024)S(1)}, f32[16384,128]{1,0:T(8,128)}) fusion(f32[128]{0:T(128)S(1)} %get-tuple-element.375, bf16[128,128]{1,0:T(8,128)(2,1)S(1)} %get-tuple-element.379, f32[16384,128]{1,0:T(8,128)S(1)} %fusion.59), kind=kOutput, calls=%fused_computation.7.clone.1 | convolution fusion | flops 559923200 | bytes 16876032 | tf_op jit(solution)/shard_map/while/body/eval_jaxpr/dot_general | solution.py:53
  179.0 1.3 compare_convert_fusion.3
  180.3 10.2 %fusion.60 = f32[16384]{0:T(1024)S(1)} fusion(bf16[16,128]{1,0:T(8,128)(2,1)S(1)} %get-tuple-element.376, bf16[128,128]{1,0:T(8,128)(2,1)S(1)} %get-tuple-element.379, f32[16384,128]{1,0:T(8,128)} %copy-done.1, f32[16384,128]{1,0:T(8,128)} %get-tuple-element.329, f32[128]{0:T(128)S(1)} %get-tuple-element.375, f32[16384]{0:T(1024)S(1)} %bitcast_multiply_fusion.3, ...), kind=kOutput, calls=%fused_computation.19.clone.1 | convolution fusion | flops 645644288 | bytes 17011264 | tf_op jit(solution)/shard_map/while/body/eval_jaxpr/dot_general | solution.py:64
  196.0 1.4 fusion.59
  197.5 7.0 %multiply_reduce_fusion.2 = (f32[16384]{0:T(1024)S(1)}, f32[16384,128]{1,0:T(8,128)}) fusion(f32[128]{0:T(128)S(1)} %get-tuple-element.375, bf16[128,128]{1,0:T(8,128)(2,1)S(1)} %get-tuple-element.379, f32[16384,128]{1,0:T(8,128)S(1)} %fusion.59), kind=kOutput, calls=%fused_computation.7.clone.1 | convolution fusion | flops 559923200 | bytes 16876032 | tf_op jit(solution)/shard_map/while/body/eval_jaxpr/dot_general | solution.py:53
  205.7 1.3 compare_convert_fusion.3
  207.0 10.2 %fusion.60 = f32[16384]{0:T(1024)S(1)} fusion(bf16[16,128]{1,0:T(8,128)(2,1)S(1)} %get-tuple-element.376, bf16[128,128]{1,0:T(8,128)(2,1)S(1)} %get-tuple-element.379, f32[16384,128]{1,0:T(8,128)} %copy-done.1, f32[16384,128]{1,0:T(8,128)} %get-tuple-element.329, f32[128]{0:T(128)S(1)} %get-tuple-element.375, f32[16384]{0:T(1024)S(1)} %bitcast_multiply_fusion.3, ...), kind=kOutput, calls=%fused_computation.19.clone.1 | convolution fusion | flops 645644288 | bytes 17011264 | tf_op jit(solution)/shard_map/while/body/eval_jaxpr/dot_general | solution.py:64
  222.7 1.4 fusion.59
  224.1 7.0 %multiply_reduce_fusion.2 = (f32[16384]{0:T(1024)S(1)}, f32[16384,128]{1,0:T(8,128)}) fusion(f32[128]{0:T(128)S(1)} %get-tuple-element.375, bf16[128,128]{1,0:T(8,128)(2,1)S(1)} %get-tuple-element.379, f32[16384,128]{1,0:T(8,128)S(1)} %fusion.59), kind=kOutput, calls=%fused_computation.7.clone.1 | convolution fusion | flops 559923200 | bytes 16876032 | tf_op jit(solution)/shard_map/while/body/eval_jaxpr/dot_general | solution.py:53
  232.4 1.3 compare_convert_fusion.3
  233.7 10.2 %fusion.60 = f32[16384]{0:T(1024)S(1)} fusion(bf16[16,128]{1,0:T(8,128)(2,1)S(1)} %get-tuple-element.376, bf16[128,128]{1,0:T(8,128)(2,1)S(1)} %get-tuple-element.379, f32[16384,128]{1,0:T(8,128)} %copy-done.1, f32[16384,128]{1,0:T(8,128)} %get-tuple-element.329, f32[128]{0:T(128)S(1)} %get-tuple-element.375, f32[16384]{0:T(1024)S(1)} %bitcast_multiply_fusion.3, ...), kind=kOutput, calls=%fused_computation.19.clone.1 | convolution fusion | flops 645644288 | bytes 17011264 | tf_op jit(solution)/shard_map/while/body/eval_jaxpr/dot_general | solution.py:64
  249.4 1.4 fusion.59
  250.8 7.0 %multiply_reduce_fusion.2 = (f32[16384]{0:T(1024)S(1)}, f32[16384,128]{1,0:T(8,128)}) fusion(f32[128]{0:T(128)S(1)} %get-tuple-element.375, bf16[128,128]{1,0:T(8,128)(2,1)S(1)} %get-tuple-element.379, f32[16384,128]{1,0:T(8,128)S(1)} %fusion.59), kind=kOutput, calls=%fused_computation.7.clone.1 | convolution fusion | flops 559923200 | bytes 16876032 | tf_op jit(solution)/shard_map/while/body/eval_jaxpr/dot_general | solution.py:53
  259.1 1.3 compare_convert_fusion.3
  260.4 10.2 %fusion.60 = f32[16384]{0:T(1024)S(1)} fusion(bf16[16,128]{1,0:T(8,128)(2,1)S(1)} %get-tuple-element.376, bf16[128,128]{1,0:T(8,128)(2,1)S(1)} %get-tuple-element.379, f32[16384,128]{1,0:T(8,128)} %copy-done.1, f32[16384,128]{1,0:T(8,128)} %get-tuple-element.329, f32[128]{0:T(128)S(1)} %get-tuple-element.375, f32[16384]{0:T(1024)S(1)} %bitcast_multiply_fusion.3, ...), kind=kOutput, calls=%fused_computation.19.clone.1 | convolution fusion | flops 645644288 | bytes 17011264 | tf_op jit(solution)/shard_map/while/body/eval_jaxpr/dot_general | solution.py:64
  271.1 3.0 %collective-permute-start.7 = (f32[3,4096]{1,0:T(4,128)S(1)}, f32[3,4096]{1,0:T(4,128)S(1)}, u32[]{:S(2)}, u32[]{:S(2)}) collective-permute-start(f32[3,4096]{1,0:T(4,128)S(1)} %get-tuple-element.240), channel_id=1, source_target_pairs={{0,31},{1,0},{2,1},{3,2},{4,3},{5,4},{6,5},{7,6},{8,7},{9,8},{10,9... | collective-permute-start | bytes 147464 | tf_op jit(solution)/shard_map/ppermute | solution.py:12
  274.1 1.5 collective-permute-start.6
  276.0 1.6 collective-permute-start.8
  277.6 2.7 collective-permute-done.8
  (162 shorter events, 44.9 us)
Async XLA Ops:
  0.0 52.6 %copy-start = (bf16[128,128]{1,0:T(8,128)(2,1)S(1)}, bf16[128,128]{1,0:T(8,128)(2,1)}, u32[]{:S(2)}) copy-start(bf16[128,128]{1,0:T(8,128)(2,1)} %param.20) | copy-start | bytes 98308
  0.0 22.2 %collective-permute-start.3 = (bf16[4096,128]{1,0:T(8,128)(2,1)}, bf16[4096,128]{1,0:T(8,128)(2,1)S(1)}, u32[]{:S(2)}, u32[]{:S(2)}) collective-permute-start(bf16[4096,128]{1,0:T(8,128)(2,1)} %param.14), channel_id=1, source_target_pairs={{0,1},{1,2},{2,3},{3,4},{4,5},{5,6},{6,7},{7,8},{8,9},{9,10},{10,1... | collective-permute-start | bytes 3145736 | tf_op jit(solution)/shard_map/ppermute | solution.py:12
  0.0 19.1 %collective-permute-start = (bf16[3,4096]{1,0:T(4,128)(2,1)}, bf16[3,4096]{1,0:T(4,128)(2,1)S(1)}, u32[]{:S(2)}, u32[]{:S(2)}) collective-permute-start(bf16[3,4096]{1,0:T(4,128)(2,1)} %param.13), channel_id=1, source_target_pairs={{0,1},{1,2},{2,3},{3,4},{4,5},{5,6},{6,7},{7,8},{8,9},{9,10},{10,1... | collective-permute-start | bytes 73736 | tf_op jit(solution)/shard_map/ppermute | solution.py:12
  2.1 29.7 %collective-permute-start.4 = (bf16[4096,128]{1,0:T(8,128)(2,1)}, bf16[4096,128]{1,0:T(8,128)(2,1)}, u32[]{:S(2)}, u32[]{:S(2)}) collective-permute-start(bf16[4096,128]{1,0:T(8,128)(2,1)} %param.14), channel_id=1, source_target_pairs={{0,32},{32,64},{64,96},{96,0},{1,33},{33,65},{65,97},{97,1},{2,34}... | collective-permute-start | bytes 3145736 | tf_op jit(solution)/shard_map/ppermute | solution.py:12
  3.6 26.6 %collective-permute-start.1 = (bf16[3,4096]{1,0:T(4,128)(2,1)}, bf16[3,4096]{1,0:T(4,128)(2,1)S(1)}, u32[]{:S(2)}, u32[]{:S(2)}) collective-permute-start(bf16[3,4096]{1,0:T(4,128)(2,1)} %param.13), channel_id=1, source_target_pairs={{0,32},{32,64},{64,96},{96,0},{1,33},{33,65},{65,97},{97,1},{2,34}... | collective-permute-start | bytes 73736 | tf_op jit(solution)/shard_map/ppermute | solution.py:12
  19.1 11.9 %collective-permute-start.2 = (bf16[3,4096]{1,0:T(4,128)(2,1)S(1)}, bf16[3,4096]{1,0:T(4,128)(2,1)S(1)}, u32[]{:S(2)}, u32[]{:S(2)}) collective-permute-start(bf16[3,4096]{1,0:T(4,128)(2,1)S(1)} %collective-permute-done), channel_id=1, source_target_pairs={{0,32},{32,64},{64,96},{96,0},{1,33},{33,65},{65,97},{97,1},{2,34}... | collective-permute-start | bytes 73736 | tf_op jit(solution)/shard_map/ppermute | solution.py:12
  22.2 30.3 %collective-permute-start.5 = (bf16[4096,128]{1,0:T(8,128)(2,1)S(1)}, bf16[4096,128]{1,0:T(8,128)(2,1)S(1)}, u32[]{:S(2)}, u32[]{:S(2)}) collective-permute-start(bf16[4096,128]{1,0:T(8,128)(2,1)S(1)} %collective-permute-done.3), channel_id=1, source_target_pairs={{0,32},{32,64},{64,96},{96,0},{1,33},{33,65},{65,97},{97,1},{2,34}... | collective-permute-start | bytes 3145736 | tf_op jit(solution)/shard_map/ppermute | solution.py:12
  31.8 25.6 %copy-start.2 = (bf16[16,128]{1,0:T(8,128)(2,1)S(1)}, bf16[16,128]{1,0:T(8,128)(2,1)}, u32[]{:S(2)}) copy-start(bf16[16,128]{1,0:T(8,128)(2,1)} %param.21) | copy-start | bytes 12292
  31.8 25.6 %copy-start.3 = (bf16[128,128]{1,0:T(8,128)(2,1)S(1)}, bf16[128,128]{1,0:T(8,128)(2,1)}, u32[]{:S(2)}) copy-start(bf16[128,128]{1,0:T(8,128)(2,1)} %param.22) | copy-start | bytes 98308
  31.8 25.6 %copy-start.4 = (s32[8]{0:T(128)S(1)}, s32[8]{0:T(128)}, u32[]{:S(2)}) copy-start(s32[8]{0:T(128)} %param.15) | copy-start | bytes 100
  31.8 25.6 %copy-start.5 = (s32[8]{0:T(128)S(1)}, s32[8]{0:T(128)}, u32[]{:S(2)}) copy-start(s32[8]{0:T(128)} %param.16) | copy-start | bytes 100
  31.8 25.6 %copy-start.6 = (s32[8]{0:T(128)S(1)}, s32[8]{0:T(128)}, u32[]{:S(2)}) copy-start(s32[8]{0:T(128)} %param.17) | copy-start | bytes 100
  31.8 25.6 %copy-start.7 = (s32[8]{0:T(128)S(1)}, s32[8]{0:T(128)}, u32[]{:S(2)}) copy-start(s32[8]{0:T(128)} %param.18) | copy-start | bytes 100
  31.9 25.6 %copy-start.8 = (f32[128]{0:T(128)S(1)}, f32[128]{0:T(128)}, u32[]{:S(2)}) copy-start(f32[128]{0:T(128)} %param.23) | copy-start | bytes 1540
  64.0 7.0 %copy-start.1 = (f32[16384,128]{1,0:T(8,128)}, f32[16384,128]{1,0:T(8,128)S(1)}, u32[]{:S(2)}) copy-start(f32[16384,128]{1,0:T(8,128)S(1)} %fusion.59) | copy-start | bytes 25165828 | tf_op jit(solution)/shard_map/while
  90.7 7.0 %copy-start.1 = (f32[16384,128]{1,0:T(8,128)}, f32[16384,128]{1,0:T(8,128)S(1)}, u32[]{:S(2)}) copy-start(f32[16384,128]{1,0:T(8,128)S(1)} %fusion.59) | copy-start | bytes 25165828 | tf_op jit(solution)/shard_map/while
  117.4 7.0 %copy-start.1 = (f32[16384,128]{1,0:T(8,128)}, f32[16384,128]{1,0:T(8,128)S(1)}, u32[]{:S(2)}) copy-start(f32[16384,128]{1,0:T(8,128)S(1)} %fusion.59) | copy-start | bytes 25165828 | tf_op jit(solution)/shard_map/while
  144.1 7.0 %copy-start.1 = (f32[16384,128]{1,0:T(8,128)}, f32[16384,128]{1,0:T(8,128)S(1)}, u32[]{:S(2)}) copy-start(f32[16384,128]{1,0:T(8,128)S(1)} %fusion.59) | copy-start | bytes 25165828 | tf_op jit(solution)/shard_map/while
  170.7 7.0 %copy-start.1 = (f32[16384,128]{1,0:T(8,128)}, f32[16384,128]{1,0:T(8,128)S(1)}, u32[]{:S(2)}) copy-start(f32[16384,128]{1,0:T(8,128)S(1)} %fusion.59) | copy-start | bytes 25165828 | tf_op jit(solution)/shard_map/while
  197.4 7.0 %copy-start.1 = (f32[16384,128]{1,0:T(8,128)}, f32[16384,128]{1,0:T(8,128)S(1)}, u32[]{:S(2)}) copy-start(f32[16384,128]{1,0:T(8,128)S(1)} %fusion.59) | copy-start | bytes 25165828 | tf_op jit(solution)/shard_map/while
  224.1 7.0 %copy-start.1 = (f32[16384,128]{1,0:T(8,128)}, f32[16384,128]{1,0:T(8,128)S(1)}, u32[]{:S(2)}) copy-start(f32[16384,128]{1,0:T(8,128)S(1)} %fusion.59) | copy-start | bytes 25165828 | tf_op jit(solution)/shard_map/while
  250.8 7.0 %copy-start.1 = (f32[16384,128]{1,0:T(8,128)}, f32[16384,128]{1,0:T(8,128)S(1)}, u32[]{:S(2)}) copy-start(f32[16384,128]{1,0:T(8,128)S(1)} %fusion.59) | copy-start | bytes 25165828 | tf_op jit(solution)/shard_map/while
  271.1 4.9 %collective-permute-start.7 = (f32[3,4096]{1,0:T(4,128)S(1)}, f32[3,4096]{1,0:T(4,128)S(1)}, u32[]{:S(2)}, u32[]{:S(2)}) collective-permute-start(f32[3,4096]{1,0:T(4,128)S(1)} %get-tuple-element.240), channel_id=1, source_target_pairs={{0,31},{1,0},{2,1},{3,2},{4,3},{5,4},{6,5},{7,6},{8,7},{9,8},{10,9... | collective-permute-start | bytes 147464 | tf_op jit(solution)/shard_map/ppermute | solution.py:12
  274.1 3.5 %collective-permute-start.6 = (f32[3,4096]{1,0:T(4,128)S(1)}, f32[3,4096]{1,0:T(4,128)S(1)}, u32[]{:S(2)}, u32[]{:S(2)}) collective-permute-start(f32[3,4096]{1,0:T(4,128)S(1)} %get-tuple-element.239), channel_id=1, source_target_pairs={{0,31},{1,0},{2,1},{3,2},{4,3},{5,4},{6,5},{7,6},{8,7},{9,8},{10,9... | collective-permute-start | bytes 147464 | tf_op jit(solution)/shard_map/ppermute | solution.py:12
  276.0 4.3 %collective-permute-start.8 = (f32[3,4096]{1,0:T(4,128)S(1)}, f32[3,4096]{1,0:T(4,128)S(1)}, u32[]{:S(2)}, u32[]{:S(2)}) collective-permute-start(f32[3,4096]{1,0:T(4,128)S(1)} %slice_add_fusion), channel_id=1, source_target_pairs={{0,96},{32,0},{64,32},{96,64},{1,97},{33,1},{65,33},{97,65},{2,98}... | collective-permute-start | bytes 147464 | tf_op jit(solution)/shard_map/ppermute | solution.py:12
where the time goes:
time: 282 us; the launch traced here: 281 us
  matrix products  155 us (55%)
  waiting for transfers between devices  44.7 us (16%)
  local copies, waits for them, and re-layouts  32.7 us (12%)
  other arithmetic  22.2 us (8%)
  starting transfers between devices  14.5 us (5%)
  loops' own time  11.2 us (4%)
    dot_general x8, matrix products, tile_gradients(): lax.dot_general(radial_weight, d_summed, (((1,), (1,)), ((), ())), prefer...  81.8 us
    dot_general x8, matrix products, tile_gradients(): pre = jnp.dot(latent, mix_weight, preferred_element_type=jnp.float32)  55.9 us
    ppermute x9, waiting for transfers between devices, passed_along(): lax.ppermute(array, axis, [(i, (i + by) % count) for i in range(count)])  44.7 us
    ppermute x9, starting transfers between devices, passed_along(): lax.ppermute(array, axis, [(i, (i + by) % count) for i in range(count)])  14.5 us
    add x16, local copies, waits for them, and re-layouts, tile_gradients(): radial + first_proj.astype(jnp.float32)[:, None, :]  12.6 us
    dot_general x8, matrix products, tile_gradients(): lax.dot_general(basis, radial_weight, (((0,), (0,)), ((), ())), preferred...  11.3 us
    another operation x1, loops' own time, on_device(): lax.fori_loop(0, tile_first.shape[0], visit, jnp.zeros((3, 4 * slot_count...  11.2 us
    convert_element_type x8, other arithmetic, live_mask(): return (jnp.arange(CELL, dtype=jnp.int32) < count).astype(jnp.float32)  10.1 us
  transfers between devices with their start and end apart: 9, of which 6 were waited for; matrix products, arithmetic and copies ran while one was open for 1% of the time, Pallas kernels for 0%

commit v1 on v0

v1 whole, which is shorter than its diff:
```python
import jax
import jax.numpy as jnp
from jax import lax
from jax.experimental import pallas as pl
from jax.experimental.pallas import tpu as pltpu
from jax.sharding import PartitionSpec as P

CELL = 128
CELLS = 32
LAT = 128
NB = 16
ROWS = 16
PIECE = 2
SLAB = CELL + 16
SPREAD = 2.8853900817779268**0.5
STEP = 6.75 / NB
F32 = jnp.float32
BF = jnp.bfloat16


def dot(a, b, dims):
    return lax.dot_general(a, b, (dims, ((), ())), preferred_element_type=F32)


def cell_slots(cell):
    return pl.ds(pl.multiple_of(cell * CELL, CELL), CELL)


def pick_kernel(ask1, ask2, ask3, pos_ref, feat_ref, out1, out2, out3):
    tiles = out1.shape[0]

    def one(t, _):
        for ask, out in ((ask1, out1), (ask2, out2), (ask3, out3)):
            slots = cell_slots(lax.rem(ask[t], CELLS))
            out[t, :CELL] = feat_ref[slots, :]
            xyz = pos_ref[:, slots].astype(F32)
            out[t, CELL:] = jnp.concatenate([xyz, jnp.zeros((13, CELL), F32)], axis=0).astype(BF)
        return 0

    lax.fori_loop(0, tiles, one, 0)


def tile_kernel(
    tf_ref, ts_ref, ca_ref, cb_ref, pos_ref, feat_ref, got1, got2, got3, wa_ref, wb_ref, wr_ref, mix_ref, ow_ref,
    own_ref, gb_ref,
    fb_ref, xb_ref, mixt_ref, back_ref, owb_ref, lead, projc, d_ref, r2_ref, diff_ref, h_s, h2_s, y_s, slope_s, z_s,
):
    W = ROWS * CELL
    PW = PIECE * CELL
    tiles = gb_ref.shape[0]

    ow = ow_ref[...]
    mix = mix_ref[...].astype(F32)
    mixt_ref[...] = (mix.T * 0.5).astype(BF)
    back_ref[:LAT] = jnp.concatenate([mix, jnp.zeros((LAT, LAT), F32)], axis=1).astype(BF)
    back_ref[LAT:] = jnp.concatenate([jnp.zeros((16, LAT), F32), jnp.ones((16, LAT), F32)], axis=1).astype(BF)
    owb_ref[...] = jnp.broadcast_to(ow, (CELL, LAT)).T

    own_ref[...] = jnp.zeros_like(own_ref)

    def fetch(t, _):
        slots = cell_slots(lax.rem(ts_ref[t], CELLS))
        source = ts_ref[t] // CELLS

        @pl.when(source == 0)
        def _():
            fb_ref[t] = feat_ref[slots, :]
            xb_ref[t] = pos_ref[:, slots].astype(F32)

        for k, got in ((1, got1), (2, got2), (3, got3)):

            @pl.when(source == k)
            def _():
                fb_ref[t] = got[t, :CELL]
                xb_ref[t] = got[t, CELL:].astype(F32)[:3]

        return 0

    lax.fori_loop(0, tiles, fetch, 0)

    def prepare(t):
        swap = cb_ref[t] < ca_ref[t]
        slots = cell_slots(tf_ref[t])
        proj_a = dot(feat_ref[slots, :], wa_ref[...], ((1,), (0,))).astype(BF).astype(F32)
        proj_b = dot(fb_ref[t], wb_ref[...], ((1,), (0,))).astype(BF).astype(F32)
        pr = jnp.where(swap, proj_b, proj_a) * 0.5
        pc = jnp.where(swap, proj_a, proj_b) * 0.5
        projc[t] = pc.T
        lead[t] = pr.reshape(CELL // ROWS, ROWS, LAT).astype(BF)
        xa = pos_ref[:, slots].astype(F32)
        xb = xb_ref[t]
        xr = jnp.where(swap, xb, xa)
        xc = jnp.where(swap, xa, xb)
        r2 = jnp.zeros((CELL, CELL), F32)
        for k in range(3):
            d = jnp.broadcast_to(xr[k : k + 1], (CELL, CELL)).T - jnp.broadcast_to(xc[k : k + 1], (CELL, CELL))
            diff_ref[t, k] = d
            r2 = r2 + d * d
        r2_ref[t] = r2 * SPREAD

    def prepare_two(u, _):
        prepare(2 * u)
        prepare(2 * u + 1)
        return 0

    lax.fori_loop(0, tiles // 2, prepare_two, 0)

    hot = lax.broadcasted_iota(jnp.int32, (ROWS, W), 0) == lax.broadcasted_iota(jnp.int32, (ROWS, W), 1) // CELL
    hot = hot.astype(F32).astype(BF)
    centers = lax.broadcasted_iota(jnp.int32, (NB, CELL), 0).astype(F32) * (STEP * SPREAD)

    def steps_of(t):
        return (jnp.minimum(ca_ref[t], cb_ref[t]) + ROWS - 1) // ROWS

    def step(it, carry):
        t1, c1, t2, c2, t3, c3, t4, c4 = carry
        rows = lambda c: pl.ds(pl.multiple_of(c * ROWS, ROWS), ROWS)
        in1 = jnp.minimum(t1, tiles - 1)
        in2 = jnp.minimum(t2, tiles - 1)
        slope_at = lax.rem(it, 2)
        z_at = lax.rem(it, 3)
        r2 = r2_ref[in1, rows(c1), :]
        lhs = jnp.concatenate([wr_ref[...] * jnp.asarray(0.5, BF), lead[in1, c1]], axis=0)
        pc = jnp.concatenate([projc[in2]] * PIECE, axis=1)
        owb = jnp.concatenate([owb_ref[...]] * PIECE, axis=1)
        cores = []
        readouts = []
        for p in range(ROWS // PIECE):
            cs = slice(p * PW, (p + 1) * PW)
            ds = (y_s[:, cs] * slope_s[slope_at, :, cs]).astype(BF)
            z = dot(wr_ref[...], ds, ((1,), (0,))) * z_s[z_at, :, cs]
            cores += [jnp.sum(z[:, i * CELL : (i + 1) * CELL], axis=0, keepdims=True) for i in range(PIECE)]
            h2 = h2_s[:, cs]
            tt = jnp.tanh(h2)
            v = owb * (1 + tt)
            act = h2 * v
            y = dot(back_ref[...], jnp.concatenate([v + act * (1 - tt), act], axis=0).astype(BF), ((1,), (0,)))
            y_s[:, cs] = y[:LAT]
            ro = y[LAT : LAT + 1]
            readouts += [ro[:, i * CELL : (i + 1) * CELL] for i in range(PIECE)]
            h = h_s[:, cs] + pc
            tt = jnp.tanh(h)
            v = 1 + tt
            act = h * v
            slope_s[slope_at, :, cs] = v + act * (1 - tt)
            h2_s[:, cs] = dot(mixt_ref[...], act.astype(BF), ((1,), (0,)))
            gs = []
            zs = []
            for i in range(p * PIECE, (p + 1) * PIECE):
                o = jnp.broadcast_to(r2[i : i + 1], (NB, CELL)) - centers
                g = jnp.exp2(-(o * o))
                gs.append(g.astype(BF))
                zs.append(g * o)
            z_s[z_at, :, cs] = jnp.concatenate(zs, axis=1)
            rhs = jnp.concatenate([jnp.concatenate(gs, axis=1), hot[:, cs]], axis=0)
            h_s[:, cs] = dot(lhs, rhs, ((0,), (0,)))
        d_ref[0, t4, rows(c4), :] = jnp.concatenate(cores, axis=0)
        d_ref[1, t3, rows(c3), :] = jnp.concatenate(readouts, axis=0)
        last = c1 + 1 >= steps_of(in1)
        return (
            jnp.where(last, jnp.minimum(t1 + 1, tiles), t1), jnp.where(last, 0, c1 + 1), t1, c1, t2, c2, t3, c3,
        )

    total = jnp.int32(3)
    for t in range(tiles):
        total = total + steps_of(t)
    none = jnp.int32(tiles)
    zero = jnp.int32(0)
    lax.fori_loop(0, total, step, (zero, zero, none, zero, none, zero, none, zero))

    def finish(t):
        ca, cb = ca_ref[t], cb_ref[t]
        swap = cb < ca
        row = lax.broadcasted_iota(jnp.int32, (CELL, CELL), 0)
        col = lax.broadcasted_iota(jnp.int32, (CELL, CELL), 1)
        live = (row < jnp.minimum(ca, cb)) & (col < jnp.maximum(ca, cb))
        env = 1 - r2_ref[t] * (0.125 / SPREAD)
        dd = env * env * (d_ref[0, t] * (-4.0 / (SPREAD * 4 * CELL))) + env * (d_ref[1, t] * (-0.25 / CELL))
        dd = jnp.where(live, 2 * dd, 0.0)
        gr = []
        gc = []
        for k in range(3):
            pull = diff_ref[t, k] * dd
            gr.append(jnp.sum(pull.T, axis=0, keepdims=True))
            gc.append(-jnp.sum(pull, axis=0, keepdims=True))
        gr = jnp.concatenate(gr, axis=0)
        gc = jnp.concatenate(gc, axis=0)
        return jnp.where(swap, gc, gr), jnp.where(swap, gr, gc)

    def put(t, ga, gb):
        own_ref[:, cell_slots(tf_ref[t])] -= ga
        gb_ref[t] = gb

        @pl.when(ts_ref[t] // CELLS == 0)
        def _():
            own_ref[:, cell_slots(lax.rem(ts_ref[t], CELLS))] -= gb

    def finish_two(u, _):
        one = finish(2 * u)
        two = finish(2 * u + 1)
        put(2 * u, *one)
        put(2 * u + 1, *two)
        return 0

    lax.fori_loop(0, tiles // 2, finish_two, 0)


def sum_kernel(ask1, ask2, ask3, own_ref, back1, back2, back3, out_ref):
    out_ref[...] = own_ref[...]

    def one(t, _):
        for k, ask, back in ((1, ask1, back1), (2, ask2, back2), (3, ask3, back3)):

            @pl.when(ask[t] // CELLS == k)
            def _():
                out_ref[:, cell_slots(lax.rem(ask[t], CELLS))] -= back[t]

        return 0

    lax.fori_loop(0, back1.shape[0], one, 0)


def on_device(
    positions, features, tile_first, tile_second, count_first, count_second, w_first, w_second, radial_weight,
    mix_weight, out_weight,
):
    n_grp = lax.axis_size("grp")
    n_dev = lax.axis_size("dev")
    tiles = tile_first.shape[0]
    smem = pl.BlockSpec(memory_space=pltpu.SMEM)
    vmem = pl.BlockSpec(memory_space=pltpu.VMEM)

    def moved(array, by_grp, by_dev):
        pairs = []
        for g in range(n_grp):
            for d in range(n_dev):
                pairs.append((g * n_dev + d, (g + by_grp) % n_grp * n_dev + (d + by_dev) % n_dev))
        return lax.ppermute(array, ("grp", "dev"), pairs)

    ways = ((0, 1), (1, 0), (1, 1))
    asks = [moved(tile_second, -g, -d) for g, d in ways]
    sent = pl.pallas_call(
        pick_kernel,
        out_shape=[jax.ShapeDtypeStruct((tiles, SLAB, LAT), BF)] * 3,
        in_specs=[smem] * 3 + [vmem] * 2,
        out_specs=[vmem] * 3,
        name="pick",
    )(*asks, positions, features)
    got = [moved(array, g, d) for array, (g, d) in zip(sent, ways)]
    W = ROWS * CELL
    own, second = pl.pallas_call(
        tile_kernel,
        out_shape=[jax.ShapeDtypeStruct(positions.shape, F32), jax.ShapeDtypeStruct((tiles, 3, CELL), F32)],
        in_specs=[smem] * 4 + [vmem] * 10,
        out_specs=[vmem] * 2,
        scratch_shapes=[
            pltpu.VMEM((tiles, CELL, LAT), BF),
            pltpu.VMEM((tiles, 3, CELL), F32),
            pltpu.VMEM((LAT, LAT), BF),
            pltpu.VMEM((LAT + 16, 2 * LAT), BF),
            pltpu.VMEM((LAT, CELL), F32),
            pltpu.VMEM((tiles, CELL // ROWS, ROWS, LAT), BF),
            pltpu.VMEM((tiles, LAT, CELL), F32),
            pltpu.VMEM((2, tiles + 1, CELL, CELL), F32),
            pltpu.VMEM((tiles, CELL, CELL), F32),
            pltpu.VMEM((tiles, 3, CELL, CELL), F32),
            pltpu.VMEM((LAT, W), F32),
            pltpu.VMEM((LAT, W), F32),
            pltpu.VMEM((LAT, W), F32),
            pltpu.VMEM((2, LAT, W), F32),
            pltpu.VMEM((3, NB, W), F32),
        ],
        compiler_params=pltpu.CompilerParams(vmem_limit_bytes=40 << 20),
        name="tiles",
    )(
        tile_first, tile_second, count_first, count_second, positions, features, *got, w_first, w_second,
        radial_weight, mix_weight, out_weight.reshape(1, LAT),
    )
    returned = [moved(second, -g, -d) for g, d in ways]
    return pl.pallas_call(
        sum_kernel,
        out_shape=jax.ShapeDtypeStruct(positions.shape, F32),
        in_specs=[smem] * 3 + [vmem] * 4,
        out_specs=vmem,
        name="sum",
    )(*asks, own, *returned)


def solution(mesh):
    each = P(("grp", "dev"))
    in_specs = (P(None, ("grp", "dev")), P(("grp", "dev"), None), each, each, each, each, P(), P(), P(), P(), P())
    return jax.shard_map(
        on_device, mesh=mesh, in_specs=in_specs, out_specs=P(None, ("grp", "dev")), check_vma=False
    )
```

time: 282 us -> 101 us (0.36)
  matrix products: 155 us -> 0 us
  Pallas kernels: 0 us -> 58.7 us
  local copies, waits for them, and re-layouts: 32.7 us -> 4.1 us
  other arithmetic: 22.2 us -> 0 us
  waiting for transfers between devices: 44.7 us -> 25.1 us
  loops' own time: 11.2 us -> 0 us
    dot_general x26 -> x0, matrix products: 155 us -> none  [the longest x8 81.8 us: tile_gradients(): lax.dot_general(radial_weight, d_summed, (((1,), (1,)), ((), ())), prefer...]
    pallas_call x0 -> x3, Pallas kernels: none -> 58.7 us  [the longest x1 54.5 us: on_device(): pl.pallas_call(tile_kernel, out_shape=[jax.ShapeDtypeStruct(positions.sha...]
    dynamic_slice x40 -> x0, local copies, waits for them, and re-layouts: 20 us -> none  [the longest x8 5.31 us: visit(): count_first[index]]
    ppermute x9, waiting for transfers between devices: 44.7 us -> 25.1 us  [moved(): return lax.ppermute(array, ('grp', 'dev'), pairs)]
    convert_element_type x17 -> x0, other arithmetic: 17.1 us -> none  [the longest x8 10.1 us: live_mask(): return (jnp.arange(CELL, dtype=jnp.int32) < count).astype(jnp.float32)]
    add x16 -> x0, local copies, waits for them, and re-layouts: 12.6 us -> none  [tile_gradients(): radial + first_proj.astype(jnp.float32)[:, None, :]]
    another operation x1 -> x0, loops' own time: 11.2 us -> none  [on_device(): lax.fori_loop(0, tile_first.shape[0], visit, jnp.zeros((3, 4 * slot_count...]
    unnamed x16 -> x36, local copies, waits for them, and re-layouts: 0.05 us -> 4.1 us
  transfers between devices with their start and end apart: 9 -> 9, of which waited for: 6 -> 7; matrix products, arithmetic and copies ran while one was open for 1% -> 0% of each run, Pallas kernels for 0% -> 0%
where the time goes in v1:
time: 101 us
  Pallas kernels  58.7 us (58%)
  waiting for transfers between devices  25.1 us (25%)
  starting transfers between devices  12.5 us (12%)
  local copies, waits for them, and re-layouts  4.1 us (4%)
    pallas_call x1, Pallas kernels, on_device(): pl.pallas_call(tile_kernel, out_shape=[jax.ShapeDtypeStruct(positions.sha...  54.5 us
    ppermute x9, waiting for transfers between devices, moved(): return lax.ppermute(array, ('grp', 'dev'), pairs)  25.1 us
    ppermute x9, starting transfers between devices, moved(): return lax.ppermute(array, ('grp', 'dev'), pairs)  12.5 us
    unnamed x36, local copies, waits for them, and re-layouts  4.1 us
    pallas_call x1, Pallas kernels, on_device(): pl.pallas_call(pick_kernel, out_shape=[jax.ShapeDtypeStruct((tiles, SLAB,...  2.35 us
  transfers between devices with their start and end apart: 9, of which 7 were waited for; matrix products, arithmetic and copies ran while one was open for 0% of the time, Pallas kernels for 0%

profile of v1, /device:TPU:0, one launch (start us, length us, event | category | flops | bytes accessed | tf_op | source)
XLA Modules:
  0.0 100.6 jit_solution(7464828656177514734)
XLA Ops:
  0.0 0.0 copy-start
  0.0 0.0 copy-start.1
  0.0 2.8 %collective-permute-start.1 = (s32[8]{0:T(128)}, s32[8]{0:T(128)S(1)}, u32[]{:S(2)}, u32[]{:S(2)}) collective-permute-start(s32[8]{0:T(128)} %ts_ref.1), channel_id=1, source_target_pairs={{0,96},{1,97},{2,98},{3,99},{4,100},{5,101},{6,102},{7,103},{8,104... | collective-permute-start | bytes 104 | tf_op jit(solution)/shard_map/ppermute | solution.py:238
  2.8 5.6 %collective-permute-start = (s32[8]{0:T(128)}, s32[8]{0:T(128)S(1)}, u32[]{:S(2)}, u32[]{:S(2)}) collective-permute-start(s32[8]{0:T(128)} %ts_ref.1), channel_id=1, source_target_pairs={{0,31},{1,0},{2,1},{3,2},{4,3},{5,4},{6,5},{7,6},{8,7},{9,8},{10,9... | collective-permute-start | bytes 104 | tf_op jit(solution)/shard_map/ppermute | solution.py:238
  8.5 1.2 %collective-permute-start.2 = (s32[8]{0:T(128)}, s32[8]{0:T(128)S(1)}, u32[]{:S(2)}, u32[]{:S(2)}) collective-permute-start(s32[8]{0:T(128)} %ts_ref.1), channel_id=1, source_target_pairs={{0,127},{1,96},{2,97},{3,98},{4,99},{5,100},{6,101},{7,102},{8,103... | collective-permute-start | bytes 104 | tf_op jit(solution)/shard_map/ppermute | solution.py:238
  9.7 0.0 collective-permute-done.1.ask2
  9.7 0.0 copy-start.15
  9.7 0.2 collective-permute-done.ask1
  9.9 0.0 copy-start.16
  9.9 1.7 %collective-permute-done.2.ask3 = s32[8]{0:T(128)S(1)} collective-permute-done((s32[8]{0:T(128)}, s32[8]{0:T(128)S(1)}, u32[]{:S(2)}, u32[]{:S(2)}) %collective-permute-start.2) | collective-permute-done | bytes 64 | tf_op jit(solution)/shard_map/ppermute | solution.py:238
  11.6 0.0 copy-done.15
  11.6 0.0 copy-done.16
  11.6 0.0 copy-start.17
  11.6 0.6 copy-done.17
  12.2 2.4 %pick.1 = (bf16[8,144,128]{2,1,0:T(8,128)(2,1)}, bf16[8,144,128]{2,1,0:T(8,128)(2,1)}, bf16[8,144,128]{2,1,0:T(8,128)(2,1)}) custom-call(s32[8]{0:T(128)} %copy-done.16, s32[8]{0:T(128)} %copy-done.15, s32[8]{0:T(128)} %copy-done.17, bf16[3,4096]{1,0:T(4,128)(2,1)} %pos_ref.3, bf16[4096,128]{1,0:T(8,128)(2,1)} %feat_ref.3), custom_call_target="tpu_custom_call" | custom-call | tf_op jit(solution)/shard_map/pick/pallas_call | solution.py:242
  14.5 0.0 copy-start.6
  14.5 0.0 collective-permute-start.3
  14.5 0.8 collective-permute-start.4
  15.4 0.0 copy-start.9
  15.4 0.1 collective-permute-start.5
  15.5 8.9 %collective-permute-done.3.got1 = bf16[8,144,128]{2,1,0:T(8,128)(2,1)S(1)} collective-permute-done((bf16[8,144,128]{2,1,0:T(8,128)(2,1)}, bf16[8,144,128]{2,1,0:T(8,128)(2,1)S(1)}, u32[]{:S(2)}, u32[]{:S(2)}) %collective-permute-start.3) | collective-permute-done | bytes 294944 | tf_op jit(solution)/shard_map/ppermute | solution.py:238
  24.3 1.6 %collective-permute-done.4.got2 = bf16[8,144,128]{2,1,0:T(8,128)(2,1)S(1)} collective-permute-done((bf16[8,144,128]{2,1,0:T(8,128)(2,1)}, bf16[8,144,128]{2,1,0:T(8,128)(2,1)S(1)}, u32[]{:S(2)}, u32[]{:S(2)}) %collective-permute-start.4) | collective-permute-done | bytes 294944 | tf_op jit(solution)/shard_map/ppermute | solution.py:238
  26.0 9.4 %collective-permute-done.5.got3 = bf16[8,144,128]{2,1,0:T(8,128)(2,1)S(1)} collective-permute-done((bf16[8,144,128]{2,1,0:T(8,128)(2,1)}, bf16[8,144,128]{2,1,0:T(8,128)(2,1)S(1)}, u32[]{:S(2)}, u32[]{:S(2)}) %collective-permute-start.5) | collective-permute-done | bytes 294944 | tf_op jit(solution)/shard_map/ppermute | solution.py:238
  35.4 0.0 copy-done
  35.4 0.0 copy-done.1
  35.4 0.0 copy-done.6
  35.4 0.0 copy-done.10
  35.4 0.0 copy-done.11
  35.4 0.0 copy-done.7
  35.4 0.0 copy-done.8
  35.4 0.0 copy-done.9
  35.4 0.0 copy-start.3
  35.4 0.7 copy-done.3
  36.2 0.8 copy-done.4
  37.0 0.8 copy-done.5
  37.7 54.5 %tiles.1 = (f32[3,4096]{1,0:T(4,128)S(1)}, f32[8,3,128]{2,1,0:T(4,128)S(1)}) custom-call(s32[8]{0:T(128)S(1)} %copy-done.8, s32[8]{0:T(128)S(1)} %copy-done.7, s32[8]{0:T(128)S(1)} %copy-done.9, s32[8]{0:T(128)S(1)} %copy-done.10, bf16[3,4096]{1,0:T(4,128)(2,1)S(1)} %copy-done.1, bf16[4096,128]{1,0:T(8,128)(2,1)S(1)} %copy-done, ...), custom_call_target="tpu_custom_call" | custom-call | tf_op jit(solution)/shard_map/tiles/pallas_call | solution.py:251
  92.2 0.0 copy-start.2
  92.2 0.6 copy-done.2
  92.8 0.0 collective-permute-start.8
  92.8 0.0 collective-permute-start.7
  92.8 1.9 %collective-permute-start.6 = (f32[8,3,128]{2,1,0:T(4,128)S(1)}, f32[8,3,128]{2,1,0:T(4,128)S(1)}, u32[]{:S(2)}, u32[]{:S(2)}) collective-permute-start(f32[8,3,128]{2,1,0:T(4,128)S(1)} %get-tuple-element.14), channel_id=1, source_target_pairs={{0,31},{1,0},{2,1},{3,2},{4,3},{5,4},{6,5},{7,6},{8,7},{9,8},{10,9... | collective-permute-start | bytes 36872 | tf_op jit(solution)/shard_map/ppermute | solution.py:238
  94.8 1.2 %collective-permute-done.8.back3 = f32[8,3,128]{2,1,0:T(4,128)S(1)} collective-permute-done((f32[8,3,128]{2,1,0:T(4,128)S(1)}, f32[8,3,128]{2,1,0:T(4,128)S(1)}, u32[]{:S(2)}, u32[]{:S(2)}) %collective-permute-start.8) | collective-permute-done | bytes 12320 | tf_op jit(solution)/shard_map/ppermute | solution.py:238
  96.0 2.1 %collective-permute-done.7.back2 = f32[8,3,128]{2,1,0:T(4,128)S(1)} collective-permute-done((f32[8,3,128]{2,1,0:T(4,128)S(1)}, f32[8,3,128]{2,1,0:T(4,128)S(1)}, u32[]{:S(2)}, u32[]{:S(2)}) %collective-permute-start.7) | collective-permute-done | bytes 12320 | tf_op jit(solution)/shard_map/ppermute | solution.py:238
  98.1 0.0 collective-permute-done.6.back1
  98.1 0.0 copy-done.12
  98.1 0.6 copy-done.13
  98.7 0.0 copy-done.14
  98.7 1.9 %sum.1 = f32[3,4096]{1,0:T(4,128)} custom-call(s32[8]{0:T(128)} %copy-done.16, s32[8]{0:T(128)} %copy-done.15, s32[8]{0:T(128)} %copy-done.17, f32[3,4096]{1,0:T(4,128)} %copy-done.2, f32[8,3,128]{2,1,0:T(4,128)} %copy-done.14, f32[8,3,128]{2,1,0:T(4,128)} %copy-done.13, f32[8,3,128]{2,1,0:T(4,128)} %copy-done.12), custom_call_target="tpu_custom_call" | custom-call | tf_op jit(solution)/shard_map/sum/pallas_call | solution.py:280
  (9 shorter events, 0.0 us)
Async XLA Ops:
  0.0 35.4 %copy-start = (bf16[4096,128]{1,0:T(8,128)(2,1)S(1)}, bf16[4096,128]{1,0:T(8,128)(2,1)}, u32[]{:S(2)}) copy-start(bf16[4096,128]{1,0:T(8,128)(2,1)} %feat_ref.3) | copy-start | bytes 3145732
  0.0 35.4 %copy-start.1 = (bf16[3,4096]{1,0:T(4,128)(2,1)S(1)}, bf16[3,4096]{1,0:T(4,128)(2,1)}, u32[]{:S(2)}) copy-start(bf16[3,4096]{1,0:T(4,128)(2,1)} %pos_ref.3) | copy-start | bytes 73732
  0.0 9.7 %collective-permute-start.1 = (s32[8]{0:T(128)}, s32[8]{0:T(128)S(1)}, u32[]{:S(2)}, u32[]{:S(2)}) collective-permute-start(s32[8]{0:T(128)} %ts_ref.1), channel_id=1, source_target_pairs={{0,96},{1,97},{2,98},{3,99},{4,100},{5,101},{6,102},{7,103},{8,104... | collective-permute-start | bytes 104 | tf_op jit(solution)/shard_map/ppermute | solution.py:238
  2.8 7.1 %collective-permute-start = (s32[8]{0:T(128)}, s32[8]{0:T(128)S(1)}, u32[]{:S(2)}, u32[]{:S(2)}) collective-permute-start(s32[8]{0:T(128)} %ts_ref.1), channel_id=1, source_target_pairs={{0,31},{1,0},{2,1},{3,2},{4,3},{5,4},{6,5},{7,6},{8,7},{9,8},{10,9... | collective-permute-start | bytes 104 | tf_op jit(solution)/shard_map/ppermute | solution.py:238
  8.5 3.1 %collective-permute-start.2 = (s32[8]{0:T(128)}, s32[8]{0:T(128)S(1)}, u32[]{:S(2)}, u32[]{:S(2)}) collective-permute-start(s32[8]{0:T(128)} %ts_ref.1), channel_id=1, source_target_pairs={{0,127},{1,96},{2,97},{3,98},{4,99},{5,100},{6,101},{7,102},{8,103... | collective-permute-start | bytes 104 | tf_op jit(solution)/shard_map/ppermute | solution.py:238
  9.7 1.9 %copy-start.15 = (s32[8]{0:T(128)}, s32[8]{0:T(128)S(1)}, u32[]{:S(2)}) copy-start(s32[8]{0:T(128)S(1)} %collective-permute-done.1.ask2) | copy-start | bytes 100
  9.9 1.7 %copy-start.16 = (s32[8]{0:T(128)}, s32[8]{0:T(128)S(1)}, u32[]{:S(2)}) copy-start(s32[8]{0:T(128)S(1)} %collective-permute-done.ask1) | copy-start | bytes 100
  11.6 0.6 copy-start.17
  14.5 20.8 %copy-start.6 = (bf16[16,128]{1,0:T(8,128)(2,1)S(1)}, bf16[16,128]{1,0:T(8,128)(2,1)}, u32[]{:S(2)}) copy-start(bf16[16,128]{1,0:T(8,128)(2,1)} %wr_ref.1) | copy-start | bytes 12292
  14.5 9.8 %collective-permute-start.3 = (bf16[8,144,128]{2,1,0:T(8,128)(2,1)}, bf16[8,144,128]{2,1,0:T(8,128)(2,1)S(1)}, u32[]{:S(2)}, u32[]{:S(2)}) collective-permute-start(bf16[8,144,128]{2,1,0:T(8,128)(2,1)} %get-tuple-element.10), channel_id=1, source_target_pairs={{0,1},{1,2},{2,3},{3,4},{4,5},{5,6},{6,7},{7,8},{8,9},{9,10},{10,1... | collective-permute-start | bytes 884744 | tf_op jit(solution)/shard_map/ppermute | solution.py:238
  14.5 11.4 %collective-permute-start.4 = (bf16[8,144,128]{2,1,0:T(8,128)(2,1)}, bf16[8,144,128]{2,1,0:T(8,128)(2,1)S(1)}, u32[]{:S(2)}, u32[]{:S(2)}) collective-permute-start(bf16[8,144,128]{2,1,0:T(8,128)(2,1)} %get-tuple-element.11), channel_id=1, source_target_pairs={{0,32},{1,33},{2,34},{3,35},{4,36},{5,37},{6,38},{7,39},{8,40},{9,... | collective-permute-start | bytes 884744 | tf_op jit(solution)/shard_map/ppermute | solution.py:238
  15.3 20.0 %copy-start.10 = (s32[8]{0:T(128)S(1)}, s32[8]{0:T(128)}, u32[]{:S(2)}) copy-start(s32[8]{0:T(128)} %cb_ref.1) | copy-start | bytes 100
  15.4 20.0 %copy-start.11 = (f32[128]{0:T(128)S(1)}, f32[128]{0:T(128)}, u32[]{:S(2)}) copy-start(f32[128]{0:T(128)} %param.21) | copy-start | bytes 1540
  15.4 20.1 %copy-start.7 = (s32[8]{0:T(128)S(1)}, s32[8]{0:T(128)}, u32[]{:S(2)}) copy-start(s32[8]{0:T(128)} %ts_ref.1) | copy-start | bytes 100
  15.4 20.1 %copy-start.8 = (s32[8]{0:T(128)S(1)}, s32[8]{0:T(128)}, u32[]{:S(2)}) copy-start(s32[8]{0:T(128)} %tf_ref.1) | copy-start | bytes 100
  15.4 20.1 %copy-start.9 = (s32[8]{0:T(128)S(1)}, s32[8]{0:T(128)}, u32[]{:S(2)}) copy-start(s32[8]{0:T(128)} %ca_ref.1) | copy-start | bytes 100
  15.4 20.0 %collective-permute-start.5 = (bf16[8,144,128]{2,1,0:T(8,128)(2,1)}, bf16[8,144,128]{2,1,0:T(8,128)(2,1)S(1)}, u32[]{:S(2)}, u32[]{:S(2)}) collective-permute-start(bf16[8,144,128]{2,1,0:T(8,128)(2,1)} %get-tuple-element.12), channel_id=1, source_target_pairs={{0,33},{1,34},{2,35},{3,36},{4,37},{5,38},{6,39},{7,40},{8,41},{9,... | collective-permute-start | bytes 884744 | tf_op jit(solution)/shard_map/ppermute | solution.py:238
  35.4 0.8 copy-start.3
  36.2 0.8 copy-start.4
  37.0 0.8 copy-start.5
  92.2 0.6 copy-start.2
  92.8 3.2 %collective-permute-start.8 = (f32[8,3,128]{2,1,0:T(4,128)S(1)}, f32[8,3,128]{2,1,0:T(4,128)S(1)}, u32[]{:S(2)}, u32[]{:S(2)}) collective-permute-start(f32[8,3,128]{2,1,0:T(4,128)S(1)} %get-tuple-element.14), channel_id=1, source_target_pairs={{0,127},{1,96},{2,97},{3,98},{4,99},{5,100},{6,101},{7,102},{8,103... | collective-permute-start | bytes 36872 | tf_op jit(solution)/shard_map/ppermute | solution.py:238
  92.8 5.3 %collective-permute-start.7 = (f32[8,3,128]{2,1,0:T(4,128)S(1)}, f32[8,3,128]{2,1,0:T(4,128)S(1)}, u32[]{:S(2)}, u32[]{:S(2)}) collective-permute-start(f32[8,3,128]{2,1,0:T(4,128)S(1)} %get-tuple-element.14), channel_id=1, source_target_pairs={{0,96},{1,97},{2,98},{3,99},{4,100},{5,101},{6,102},{7,103},{8,104... | collective-permute-start | bytes 36872 | tf_op jit(solution)/shard_map/ppermute | solution.py:238
  92.8 5.3 %collective-permute-start.6 = (f32[8,3,128]{2,1,0:T(4,128)S(1)}, f32[8,3,128]{2,1,0:T(4,128)S(1)}, u32[]{:S(2)}, u32[]{:S(2)}) collective-permute-start(f32[8,3,128]{2,1,0:T(4,128)S(1)} %get-tuple-element.14), channel_id=1, source_target_pairs={{0,31},{1,0},{2,1},{3,2},{4,3},{5,4},{6,5},{7,6},{8,7},{9,8},{10,9... | collective-permute-start | bytes 36872 | tf_op jit(solution)/shard_map/ppermute | solution.py:238
  96.0 2.1 %copy-start.12 = (f32[8,3,128]{2,1,0:T(4,128)}, f32[8,3,128]{2,1,0:T(4,128)S(1)}, u32[]{:S(2)}) copy-start(f32[8,3,128]{2,1,0:T(4,128)S(1)} %collective-permute-done.8.back3) | copy-start | bytes 36868
  98.1 0.6 copy-start.13
  98.1 0.6 copy-start.14

commit v2 on v1

v2 whole, which is shorter than its diff:
```python
import functools

import jax
import jax.numpy as jnp
from jax import lax
from jax.experimental import pallas as pl
from jax.experimental.pallas import tpu as pltpu
from jax.sharding import PartitionSpec as P

CELL = 128
CELLS = 32
LAT = 128
NB = 16
ROWS = 16
SUB = 8
PIECE = 2
WAYS = ((0, 1), (1, 0), (1, 1))
MESH = pl.DeviceIdType.MESH
SPREAD = 2.8853900817779268**0.5
STEP = 6.75 / NB
F32 = jnp.float32
BF = jnp.bfloat16


def dot(a, b, dims):
    return lax.dot_general(a, b, (dims, ((), ())), preferred_element_type=F32)


def cell_slots(cell):
    return pl.ds(pl.multiple_of(cell * CELL, CELL), CELL)


def other(by_grp, by_dev):
    g = lax.axis_index("grp") + by_grp
    d = lax.axis_index("dev") + by_dev
    n_grp = lax.axis_size("grp")
    n_dev = lax.axis_size("dev")
    return lax.rem(g + n_grp, n_grp), lax.rem(d + n_dev, n_dev)


def fetch_kernel(
    n_tiles, ts_ref, pos_ref, feat_ref, ask_ref, got_ref, gotpos_ref,
    mine, numbers, out_ref, ask_send, ask_recv, local_sem, feat_send, feat_recv, pos_send, pos_recv,
):
    barrier = pltpu.get_barrier_semaphore()
    for g, d in WAYS:
        pl.semaphore_signal(barrier, inc=1, device_id=other(g, d), device_id_type=MESH)
        pl.semaphore_signal(barrier, inc=1, device_id=other(-g, -d), device_id_type=MESH)
    for t in range(n_tiles):
        mine[t : t + 1, :] = jnp.full((1, CELL), ts_ref[t], jnp.int32)
    pl.semaphore_wait(barrier, 2 * len(WAYS))

    asks = []
    for w, (g, d) in enumerate(WAYS):
        copy = pltpu.make_async_remote_copy(
            src_ref=mine, dst_ref=ask_ref.at[w], send_sem=ask_send.at[w], recv_sem=ask_recv.at[w],
            device_id=other(-g, -d), device_id_type=MESH,
        )
        copy.start()
        asks.append(copy)
    sent = []
    for w, (g, d) in enumerate(WAYS):
        copy = pltpu.make_async_remote_copy(
            src_ref=pos_ref, dst_ref=gotpos_ref.at[w], send_sem=pos_send.at[w], recv_sem=pos_recv.at[w],
            device_id=other(g, d), device_id_type=MESH,
        )
        copy.start()
        sent.append(copy)
    for w in (2, 1, 0):
        asks[w].wait_recv()
        local = pltpu.make_async_copy(ask_ref.at[w], numbers.at[w], local_sem.at[w])
        local.start()
        local.wait()
        for t in range(n_tiles):
            out_ref[w, t] = feat_ref[lax.rem(numbers[w, t, 0], CELLS)]
        copy = pltpu.make_async_remote_copy(
            src_ref=out_ref.at[w], dst_ref=got_ref.at[w], send_sem=feat_send.at[w], recv_sem=feat_recv.at[w],
            device_id=other(*WAYS[w]), device_id_type=MESH,
        )
        copy.start()
        sent.append(copy)
    for copy in asks:
        copy.wait_send()
    for copy in sent:
        copy.wait()


def tile_kernel(
    tf_ref, ts_ref, ca_ref, cb_ref, pos_ref, feat_ref, got_ref, gotpos_ref, wa_ref, wb_ref, wr_ref, mix_ref, ow_ref,
    own_ref, gb_ref,
    fa_ref, fb_ref, xb_ref, mixt_ref, owb_ref, lead, projc, d_ref, r2_ref, diff_ref, h_s, h2_s, y_s, slope_s, z_s,
    sem_a, sem_b,
):
    W = ROWS * CELL
    PW = PIECE * CELL
    tiles = gb_ref.shape[0]

    for t in range(tiles):
        pltpu.make_async_copy(feat_ref.at[cell_slots(tf_ref[t])], fa_ref.at[t], sem_a.at[t]).start()
        slots = cell_slots(lax.rem(ts_ref[t], CELLS))
        source = ts_ref[t] // CELLS

        @pl.when(source == 0)
        def _():
            pltpu.make_async_copy(feat_ref.at[slots], fb_ref.at[t], sem_b.at[t]).start()
            xb_ref[t] = pos_ref[:, slots].astype(F32)

        @pl.when(source > 0)
        def _():
            pltpu.make_async_copy(got_ref.at[source - 1, t], fb_ref.at[t], sem_b.at[t]).start()
            xb_ref[t] = gotpos_ref[source - 1, :, slots].astype(F32)

    mixt_ref[...] = (mix_ref[...].astype(F32).T * 0.5).astype(BF)
    owb_ref[...] = jnp.broadcast_to(ow_ref[...], (CELL, LAT)).T
    own_ref[...] = jnp.zeros_like(own_ref)
    for t in range(tiles):
        pltpu.make_async_copy(feat_ref.at[pl.ds(0, CELL)], fa_ref.at[t], sem_a.at[t]).wait()
        pltpu.make_async_copy(feat_ref.at[pl.ds(0, CELL)], fb_ref.at[t], sem_b.at[t]).wait()

    def prepare(t):
        swap = cb_ref[t] < ca_ref[t]
        slots = cell_slots(tf_ref[t])
        proj_a = dot(fa_ref[t], wa_ref[...], ((1,), (0,))).astype(BF).astype(F32)
        proj_b = dot(fb_ref[t], wb_ref[...], ((1,), (0,))).astype(BF).astype(F32)
        pr = jnp.where(swap, proj_b, proj_a) * 0.5
        pc = jnp.where(swap, proj_a, proj_b) * 0.5
        projc[t] = pc.T
        groups = pr.reshape(CELL // SUB, SUB, LAT)
        lead[t] = jnp.concatenate([groups, jnp.zeros_like(groups)], axis=1).astype(BF)
        xa = pos_ref[:, slots].astype(F32)
        xb = xb_ref[t]
        xr = jnp.where(swap, xb, xa)
        xc = jnp.where(swap, xa, xb)
        r2 = jnp.zeros((CELL, CELL), F32)
        for k in range(3):
            d = jnp.broadcast_to(xr[k : k + 1], (CELL, CELL)).T - jnp.broadcast_to(xc[k : k + 1], (CELL, CELL))
            diff_ref[t, k] = d
            r2 = r2 + d * d
        r2_ref[t] = r2 * SPREAD

    def prepare_two(u, _):
        prepare(2 * u)
        prepare(2 * u + 1)
        return 0

    lax.fori_loop(0, tiles // 2, prepare_two, 0)

    hot = lax.broadcasted_iota(jnp.int32, (16, SUB * CELL), 0)
    hot = hot == lax.broadcasted_iota(jnp.int32, (16, SUB * CELL), 1) // CELL
    hot = hot.astype(F32).astype(BF)
    centers = lax.broadcasted_iota(jnp.int32, (NB, CELL), 0).astype(F32) * (STEP * SPREAD)
    n_sub = ROWS // SUB
    per_sub = SUB // PIECE

    def subs_of(t):
        return (jnp.minimum(ca_ref[t], cb_ref[t]) + SUB - 1) // SUB

    def following(place):
        places = []
        for _ in range(n_sub):
            t, c = place
            last = c + 1 >= subs_of(jnp.minimum(t, tiles - 1))
            place = jnp.where(last, jnp.minimum(t + 1, tiles), t), jnp.where(last, 0, c + 1)
            places.append(place)
        return tuple(places)

    def step(it, carry):
        at1, at2, at3, at4 = carry
        rows = lambda c: pl.ds(pl.multiple_of(c * SUB, SUB), SUB)
        slope_at = lax.rem(it, 2)
        z_at = lax.rem(it, 3)
        owb = jnp.concatenate([owb_ref[...]] * PIECE, axis=1)
        for p in range(ROWS // PIECE):
            cs = slice(p * PW, (p + 1) * PW)
            q = p % per_sub
            if q == 0:
                (t1, c1), (t2, _), (t3, c3), (t4, c4) = (at[p // per_sub] for at in carry)
                in1 = jnp.minimum(t1, tiles - 1)
                r2 = r2_ref[in1, rows(c1), :]
                lhs = jnp.concatenate([wr_ref[...] * jnp.asarray(0.5, BF), lead[in1, c1]], axis=0)
                pc = jnp.concatenate([projc[jnp.minimum(t2, tiles - 1)]] * PIECE, axis=1)
                cores = []
                readouts = []
            ds = (y_s[:, cs] * slope_s[slope_at, :, cs]).astype(BF)
            z = dot(wr_ref[...], ds, ((1,), (0,))) * z_s[z_at, :, cs]
            cores += [jnp.sum(z[:, i * CELL : (i + 1) * CELL], axis=0, keepdims=True) for i in range(PIECE)]
            h2 = h2_s[:, cs]
            tt = jnp.tanh(h2)
            v = owb * (1 + tt)
            act = h2 * v
            y_s[:, cs] = dot(mix_ref[...], (v + act * (1 - tt)).astype(BF), ((1,), (0,)))
            ro = jnp.sum(act, axis=0, keepdims=True)
            readouts += [ro[:, i * CELL : (i + 1) * CELL] for i in range(PIECE)]
            h = h_s[:, cs] + pc
            tt = jnp.tanh(h)
            v = 1 + tt
            act = h * v
            slope_s[slope_at, :, cs] = v + act * (1 - tt)
            h2_s[:, cs] = dot(mixt_ref[...], act.astype(BF), ((1,), (0,)))
            gs = []
            zs = []
            for i in range(q * PIECE, (q + 1) * PIECE):
                o = jnp.broadcast_to(r2[i : i + 1], (NB, CELL)) - centers
                g = jnp.exp2(-(o * o))
                gs.append(g.astype(BF))
                zs.append(g * o)
            z_s[z_at, :, cs] = jnp.concatenate(zs, axis=1)
            rhs = jnp.concatenate([jnp.concatenate(gs, axis=1), hot[:, q * PW : (q + 1) * PW]], axis=0)
            h_s[:, cs] = dot(lhs, rhs, ((0,), (0,)))
            if q == per_sub - 1:
                d_ref[0, t4, rows(c4), :] = jnp.concatenate(cores, axis=0)
                d_ref[1, t3, rows(c3), :] = jnp.concatenate(readouts, axis=0)
        return following(at1[-1]), at1, at2, at3

    total = jnp.int32(0)
    for t in range(tiles):
        total = total + subs_of(t)
    zero = jnp.int32(0)
    start = (zero, zero)
    start = ((start,) + following(start))[:n_sub]
    idle = ((jnp.int32(tiles), zero),) * n_sub
    lax.fori_loop(0, (total + n_sub - 1) // n_sub + 3, step, (start, idle, idle, idle))

    def finish(t):
        ca, cb = ca_ref[t], cb_ref[t]
        swap = cb < ca
        row = lax.broadcasted_iota(jnp.int32, (CELL, CELL), 0)
        col = lax.broadcasted_iota(jnp.int32, (CELL, CELL), 1)
        live = (row < jnp.minimum(ca, cb)) & (col < jnp.maximum(ca, cb))
        env = 1 - r2_ref[t] * (0.125 / SPREAD)
        dd = env * env * (d_ref[0, t] * (-4.0 / (SPREAD * 4 * CELL))) + env * (d_ref[1, t] * (-0.25 / CELL))
        dd = jnp.where(live, 2 * dd, 0.0)
        gr = []
        gc = []
        for k in range(3):
            pull = diff_ref[t, k] * dd
            gr.append(jnp.sum(pull.T, axis=0, keepdims=True))
            gc.append(-jnp.sum(pull, axis=0, keepdims=True))
        gr = jnp.concatenate(gr, axis=0)
        gc = jnp.concatenate(gc, axis=0)
        return jnp.where(swap, gc, gr), jnp.where(swap, gr, gc)

    def put(t, ga, gb):
        own_ref[:, cell_slots(tf_ref[t])] -= ga
        gb_ref[t] = gb

        @pl.when(ts_ref[t] // CELLS == 0)
        def _():
            own_ref[:, cell_slots(lax.rem(ts_ref[t], CELLS))] -= gb

    def finish_two(u, _):
        one = finish(2 * u)
        two = finish(2 * u + 1)
        put(2 * u, *one)
        put(2 * u + 1, *two)
        return 0

    lax.fori_loop(0, tiles // 2, finish_two, 0)


def return_kernel(n_tiles, ask_ref, own_ref, second_ref, out_ref, back_ref, send_sem, recv_sem):
    barrier = pltpu.get_barrier_semaphore()
    for g, d in WAYS:
        pl.semaphore_signal(barrier, inc=1, device_id=other(g, d), device_id_type=MESH)
    pl.semaphore_wait(barrier, len(WAYS))
    copies = []
    for w, (g, d) in enumerate(WAYS):
        copy = pltpu.make_async_remote_copy(
            src_ref=second_ref, dst_ref=back_ref.at[w], send_sem=send_sem.at[w], recv_sem=recv_sem.at[w],
            device_id=other(-g, -d), device_id_type=MESH,
        )
        copy.start()
        copies.append(copy)
    for copy in copies:
        copy.wait()

    def one(c, _):
        slots = cell_slots(c)
        total = own_ref[:, slots]
        for w in range(len(WAYS)):
            for t in range(n_tiles):
                total -= jnp.where(ask_ref[w, t : t + 1, :] == (w + 1) * CELLS + c, back_ref[w, t], 0.0)
        out_ref[:, slots] = total
        return 0

    lax.fori_loop(0, CELLS, one, 0)


def on_device(
    positions, features, tile_first, tile_second, count_first, count_second, w_first, w_second, radial_weight,
    mix_weight, out_weight,
):
    tiles = tile_first.shape[0]
    smem = pl.BlockSpec(memory_space=pltpu.SMEM)
    vmem = pl.BlockSpec(memory_space=pltpu.VMEM)

    anywhere = pl.BlockSpec(memory_space=pl.ANY)
    dma = pltpu.SemaphoreType.DMA
    n = len(WAYS)
    ask, got, got_pos = pl.pallas_call(
        functools.partial(fetch_kernel, tiles),
        out_shape=[
            jax.ShapeDtypeStruct((n, tiles, CELL), jnp.int32),
            jax.ShapeDtypeStruct((n, tiles, CELL, LAT), BF),
            jax.ShapeDtypeStruct((n, *positions.shape), BF),
        ],
        in_specs=[smem, vmem, vmem],
        out_specs=[vmem, anywhere, vmem],
        scratch_shapes=[
            pltpu.VMEM((tiles, CELL), jnp.int32),
            pltpu.SMEM((n, tiles, CELL), jnp.int32),
            pltpu.VMEM((n, tiles, CELL, LAT), BF),
        ]
        + [dma((n,))] * 7,
        compiler_params=pltpu.CompilerParams(collective_id=0, has_side_effects=True),
        name="fetch",
    )(tile_second, positions, features.reshape(-1, CELL, LAT))
    W = ROWS * CELL
    own, second = pl.pallas_call(
        tile_kernel,
        out_shape=[jax.ShapeDtypeStruct(positions.shape, F32), jax.ShapeDtypeStruct((tiles, 3, CELL), F32)],
        in_specs=[smem] * 4 + [vmem, anywhere, anywhere] + [vmem] * 6,
        out_specs=[vmem] * 2,
        scratch_shapes=[
            pltpu.VMEM((tiles, CELL, LAT), BF),
            pltpu.VMEM((tiles, CELL, LAT), BF),
            pltpu.VMEM((tiles, 3, CELL), F32),
            pltpu.VMEM((LAT, LAT), BF),
            pltpu.VMEM((LAT, CELL), F32),
            pltpu.VMEM((tiles, CELL // SUB, 16, LAT), BF),
            pltpu.VMEM((tiles, LAT, CELL), F32),
            pltpu.VMEM((2, tiles + 1, CELL, CELL), F32),
            pltpu.VMEM((tiles, CELL, CELL), F32),
            pltpu.VMEM((tiles, 3, CELL, CELL), F32),
            pltpu.VMEM((LAT, W), F32),
            pltpu.VMEM((LAT, W), F32),
            pltpu.VMEM((LAT, W), F32),
            pltpu.VMEM((2, LAT, W), F32),
            pltpu.VMEM((3, NB, W), F32),
            dma((tiles,)),
            dma((tiles,)),
        ],
        compiler_params=pltpu.CompilerParams(vmem_limit_bytes=40 << 20),
        name="tiles",
    )(
        tile_first, tile_second, count_first, count_second, positions, features, got, got_pos, w_first, w_second,
        radial_weight, mix_weight, out_weight.reshape(1, LAT),
    )
    return pl.pallas_call(
        functools.partial(return_kernel, tiles),
        out_shape=jax.ShapeDtypeStruct(positions.shape, F32),
        in_specs=[vmem] * 3,
        out_specs=vmem,
        scratch_shapes=[pltpu.VMEM((n, tiles, 3, CELL), F32), dma((n,)), dma((n,))],
        compiler_params=pltpu.CompilerParams(collective_id=1, has_side_effects=True),
        name="return",
    )(ask, own, second)


def solution(mesh):
    each = P(("grp", "dev"))
    in_specs = (P(None, ("grp", "dev")), P(("grp", "dev"), None), each, each, each, each, P(), P(), P(), P(), P())
    return jax.shard_map(
        on_device, mesh=mesh, in_specs=in_specs, out_specs=P(None, ("grp", "dev")), check_vma=False
    )
```

time: 101 us -> 82.2 us (0.81)
  the two profiles are of different devices: /device:TPU:0 before, /device:TPU:35 now
where the time goes in v2:
time: 82.2 us; the launch traced here: 81.7 us
  Pallas kernels  73.9 us (90%)
  local copies, waits for them, and re-layouts  7.65 us (9%)
    pallas_call x1, Pallas kernels, on_device(): pl.pallas_call(tile_kernel, out_shape=[jax.ShapeDtypeStruct(positions.sha...  34.4 us
    pallas_call x1, Pallas kernels, on_device(): pl.pallas_call(functools.partial(fetch_kernel, tiles), out_shape=[jax.Sha...  21.8 us
    pallas_call x1, Pallas kernels, on_device(): pl.pallas_call(functools.partial(return_kernel, tiles), out_shape=jax.Sha...  17.8 us
    unnamed x31, local copies, waits for them, and re-layouts  7.65 us

profile of v2, /device:TPU:35, one launch (start us, length us, event | category | flops | bytes accessed | tf_op | source)
XLA Modules:
  0.0 81.7 jit_solution(16076997294245265058)
XLA Ops:
  0.0 0.0 copy-start
  0.0 0.0 copy-start.2
  0.0 0.0 copy-start.13
  0.0 0.0 copy-start.14
  0.0 21.8 %fetch.1 = (s32[3,8,128]{2,1,0:T(8,128)}, bf16[3,8,128,128]{3,2,1,0:T(8,128)(2,1)}, bf16[3,3,4096]{2,1,0:T(4,128)(2,1)}) custom-call(s32[8]{0:T(128)} %ts_ref.3, bf16[3,4096]{1,0:T(4,128)(2,1)} %pos_ref.3, bf16[32,128,128]{2,1,0:T(8,128)(2,1)} %bitcast.2), custom_call_target="tpu_custom_call" | custom-call | tf_op jit(solution)/shard_map/fetch/pallas_call | solution.py:300
  21.8 0.0 copy-start.9
  21.9 0.0 copy-start.10
  21.9 0.0 copy-start.11
  21.9 0.0 copy-start.12
  21.9 0.0 copy-done
  21.9 0.0 copy-done.2
  21.9 0.0 copy-done.13
  21.9 0.0 copy-done.14
  21.9 0.6 copy-done.9
  22.5 0.0 copy-done.10
  22.5 0.0 copy-done.11
  22.5 0.0 copy-done.12
  22.5 0.0 copy-start.1
  22.6 1.1 %copy-done.1 = bf16[3,8,128,128]{3,2,1,0:T(8,128)(2,1)S(1)} copy-done((bf16[3,8,128,128]{3,2,1,0:T(8,128)(2,1)S(1)}, bf16[3,8,128,128]{3,2,1,0:T(8,128)(2,1)}, u32[]{:S(2)}) %copy-start.1) | copy-done | bytes 786456
  23.7 0.0 copy-start.3
  23.7 0.9 %copy-done.3 = bf16[3,3,4096]{2,1,0:T(4,128)(2,1)S(1)} copy-done((bf16[3,3,4096]{2,1,0:T(4,128)(2,1)S(1)}, bf16[3,3,4096]{2,1,0:T(4,128)(2,1)}, u32[]{:S(2)}) %copy-start.3) | copy-done | bytes 73752
  24.6 0.0 copy-start.5
  24.6 0.8 copy-done.5
  25.3 0.0 copy-start.6
  25.3 0.8 copy-done.6
  26.1 0.0 copy-start.7
  26.1 0.8 copy-done.7
  26.9 34.4 %tiles.1 = (f32[3,4096]{1,0:T(4,128)S(1)}, f32[8,3,128]{2,1,0:T(4,128)S(1)}) custom-call(s32[8]{0:T(128)S(1)} %copy-done.11, s32[8]{0:T(128)S(1)} %copy-done.10, s32[8]{0:T(128)S(1)} %copy-done.12, s32[8]{0:T(128)S(1)} %copy-done.13, bf16[3,4096]{1,0:T(4,128)(2,1)S(1)} %copy-done.2, bf16[4096,128]{1,0:T(8,128)(2,1)S(1)} %copy-done, ...), custom_call_target="tpu_custom_call" | custom-call | tf_op jit(solution)/shard_map/tiles/pallas_call | solution.py:319
  61.2 0.0 copy-start.4
  61.2 0.6 copy-done.4
  61.8 0.0 copy-start.8
  61.9 0.6 copy-done.8
  62.4 17.8 %return.1 = f32[3,4096]{1,0:T(4,128)} custom-call(s32[3,8,128]{2,1,0:T(8,128)} %get-tuple-element.10.ask_ref, f32[3,4096]{1,0:T(4,128)} %copy-done.4, f32[8,3,128]{2,1,0:T(4,128)} %copy-done.8), custom_call_target="tpu_custom_call" | custom-call | tf_op jit(solution)/shard_map/return/pallas_call | solution.py:349
  80.2 1.5 %copy.13 = f32[3,4096]{1,0:T(4,128)} copy(f32[3,4096]{1,0:T(4,128)} %return.1) | data formatting | bytes 98304
Async XLA Ops:
  0.0 21.9 %copy-start = (bf16[4096,128]{1,0:T(8,128)(2,1)S(1)}, bf16[4096,128]{1,0:T(8,128)(2,1)}, u32[]{:S(2)}) copy-start(bf16[4096,128]{1,0:T(8,128)(2,1)} %feat_ref.1) | copy-start | bytes 3145732
  0.0 21.9 %copy-start.2 = (bf16[3,4096]{1,0:T(4,128)(2,1)S(1)}, bf16[3,4096]{1,0:T(4,128)(2,1)}, u32[]{:S(2)}) copy-start(bf16[3,4096]{1,0:T(4,128)(2,1)} %pos_ref.3) | copy-start | bytes 73732
  0.0 21.9 %copy-start.13 = (s32[8]{0:T(128)S(1)}, s32[8]{0:T(128)}, u32[]{:S(2)}) copy-start(s32[8]{0:T(128)} %cb_ref.1) | copy-start | bytes 100
  0.0 21.9 %copy-start.14 = (f32[128]{0:T(128)S(1)}, f32[128]{0:T(128)}, u32[]{:S(2)}) copy-start(f32[128]{0:T(128)} %param.21) | copy-start | bytes 1540
  21.8 0.7 copy-start.9
  21.9 0.7 copy-start.10
  21.9 0.7 copy-start.11
  21.9 0.7 copy-start.12
  22.5 1.1 %copy-start.1 = (bf16[3,8,128,128]{3,2,1,0:T(8,128)(2,1)S(1)}, bf16[3,8,128,128]{3,2,1,0:T(8,128)(2,1)}, u32[]{:S(2)}) copy-start(bf16[3,8,128,128]{3,2,1,0:T(8,128)(2,1)} %get-tuple-element.11.got_ref) | copy-start | bytes 2359300
  23.7 0.9 %copy-start.3 = (bf16[3,3,4096]{2,1,0:T(4,128)(2,1)S(1)}, bf16[3,3,4096]{2,1,0:T(4,128)(2,1)}, u32[]{:S(2)}) copy-start(bf16[3,3,4096]{2,1,0:T(4,128)(2,1)} %get-tuple-element.12.gotpos_ref) | copy-start | bytes 221188
  24.6 0.8 copy-start.5
  25.3 0.8 copy-start.6
  26.1 0.8 copy-start.7
  61.2 0.6 copy-start.4
  61.8 0.6 copy-start.8

commit v3 on v2

--- a/solution.py
+++ b/solution.py
@@ -39,9 +39,11 @@
 
 
 def fetch_kernel(
-    n_tiles, ts_ref, pos_ref, feat_ref, ask_ref, got_ref, gotpos_ref,
-    mine, numbers, out_ref, ask_send, ask_recv, local_sem, feat_send, feat_recv, pos_send, pos_recv,
+    n_tiles, ts_ref, pos_ref, feat_any, ask_ref, got_ref, gotpos_ref,
+    feat_ref, feat_sem, mine, numbers, out_ref, ask_send, ask_recv, local_sem, feat_send, feat_recv, pos_send, pos_recv,
 ):
+    features = pltpu.make_async_copy(feat_any, feat_ref, feat_sem)
+    features.start()
     barrier = pltpu.get_barrier_semaphore()
     for g, d in WAYS:
         pl.semaphore_signal(barrier, inc=1, device_id=other(g, d), device_id_type=MESH)
@@ -66,6 +68,7 @@
         )
         copy.start()
         sent.append(copy)
+    features.wait()
     for w in (2, 1, 0):
         asks[w].wait_recv()
         local = pltpu.make_async_copy(ask_ref.at[w], numbers.at[w], local_sem.at[w])
@@ -86,15 +89,23 @@
 
 
 def tile_kernel(
-    tf_ref, ts_ref, ca_ref, cb_ref, pos_ref, feat_ref, got_ref, gotpos_ref, wa_ref, wb_ref, wr_ref, mix_ref, ow_ref,
+    tf_ref, ts_ref, ca_ref, cb_ref, pos_any, feat_ref, got_ref, gotpos_any, wa_any, wb_any, wr_any, mix_any, ow_any,
     own_ref, gb_ref,
+    pos_ref, gotpos_ref, wa_ref, wb_ref, wr_ref, mix_ref, ow_ref,
     fa_ref, fb_ref, xb_ref, mixt_ref, owb_ref, lead, projc, d_ref, r2_ref, diff_ref, h_s, h2_s, y_s, slope_s, z_s,
-    sem_a, sem_b,
+    sem_a, sem_b, sem_c,
 ):
     W = ROWS * CELL
     PW = PIECE * CELL
     tiles = gb_ref.shape[0]
 
+    loads = []
+    for src, dst in (
+        (pos_any, pos_ref), (gotpos_any, gotpos_ref), (wa_any, wa_ref), (wb_any, wb_ref), (wr_any, wr_ref),
+        (mix_any, mix_ref), (ow_any, ow_ref),
+    ):
+        loads.append(pltpu.make_async_copy(src, dst, sem_c.at[len(loads)]))
+        loads[-1].start()
     for t in range(tiles):
         pltpu.make_async_copy(feat_ref.at[cell_slots(tf_ref[t])], fa_ref.at[t], sem_a.at[t]).start()
         slots = cell_slots(lax.rem(ts_ref[t], CELLS))
@@ -103,13 +114,18 @@
         @pl.when(source == 0)
         def _():
             pltpu.make_async_copy(feat_ref.at[slots], fb_ref.at[t], sem_b.at[t]).start()
-            xb_ref[t] = pos_ref[:, slots].astype(F32)
 
         @pl.when(source > 0)
         def _():
             pltpu.make_async_copy(got_ref.at[source - 1, t], fb_ref.at[t], sem_b.at[t]).start()
-            xb_ref[t] = gotpos_ref[source - 1, :, slots].astype(F32)
-
+
+    for load in loads:
+        load.wait()
+    for t in range(tiles):
+        slots = cell_slots(lax.rem(ts_ref[t], CELLS))
+        source = ts_ref[t] // CELLS
+        came = gotpos_ref[jnp.maximum(source - 1, 0), :, slots].astype(F32)
+        xb_ref[t] = jnp.where(source == 0, pos_ref[:, slots].astype(F32), came)
     mixt_ref[...] = (mix_ref[...].astype(F32).T * 0.5).astype(BF)
     owb_ref[...] = jnp.broadcast_to(ow_ref[...], (CELL, LAT)).T
     own_ref[...] = jnp.zeros_like(own_ref)
@@ -182,21 +198,19 @@
                 cores = []
                 readouts = []
             ds = (y_s[:, cs] * slope_s[slope_at, :, cs]).astype(BF)
-            z = dot(wr_ref[...], ds, ((1,), (0,))) * z_s[z_at, :, cs]
-            cores += [jnp.sum(z[:, i * CELL : (i + 1) * CELL], axis=0, keepdims=True) for i in range(PIECE)]
+            z = z_s[z_at, :, cs]
             h2 = h2_s[:, cs]
             tt = jnp.tanh(h2)
             v = owb * (1 + tt)
             act = h2 * v
-            y_s[:, cs] = dot(mix_ref[...], (v + act * (1 - tt)).astype(BF), ((1,), (0,)))
             ro = jnp.sum(act, axis=0, keepdims=True)
-            readouts += [ro[:, i * CELL : (i + 1) * CELL] for i in range(PIECE)]
+            back = (v + act * (1 - tt)).astype(BF)
             h = h_s[:, cs] + pc
             tt = jnp.tanh(h)
             v = 1 + tt
             act = h * v
             slope_s[slope_at, :, cs] = v + act * (1 - tt)
-            h2_s[:, cs] = dot(mixt_ref[...], act.astype(BF), ((1,), (0,)))
+            latent = act.astype(BF)
             gs = []
             zs = []
             for i in range(q * PIECE, (q + 1) * PIECE):
@@ -206,7 +220,13 @@
                 zs.append(g * o)
             z_s[z_at, :, cs] = jnp.concatenate(zs, axis=1)
             rhs = jnp.concatenate([jnp.concatenate(gs, axis=1), hot[:, q * PW : (q + 1) * PW]], axis=0)
+            y_s[:, cs] = dot(mix_ref[...], back, ((1,), (0,)))
             h_s[:, cs] = dot(lhs, rhs, ((0,), (0,)))
+            z = dot(wr_ref[...], ds, ((1,), (0,))) * z
+            h2_s[:, cs] = dot(mixt_ref[...], latent, ((1,), (0,)))
+            for i in range(PIECE):
+                cores.append(jnp.sum(z[:, i * CELL : (i + 1) * CELL], axis=0, keepdims=True))
+                readouts.append(ro[:, i * CELL : (i + 1) * CELL])
             if q == per_sub - 1:
                 d_ref[0, t4, rows(c4), :] = jnp.concatenate(cores, axis=0)
                 d_ref[1, t3, rows(c3), :] = jnp.concatenate(readouts, axis=0)
@@ -304,9 +324,11 @@
             jax.ShapeDtypeStruct((n, tiles, CELL, LAT), BF),
             jax.ShapeDtypeStruct((n, *positions.shape), BF),
         ],
-        in_specs=[smem, vmem, vmem],
-        out_specs=[vmem, anywhere, vmem],
+        in_specs=[smem, anywhere, anywhere],
+        out_specs=[vmem, anywhere, anywhere],
         scratch_shapes=[
+            pltpu.VMEM((CELLS, CELL, LAT), BF),
+            dma(()),
             pltpu.VMEM((tiles, CELL), jnp.int32),
             pltpu.SMEM((n, tiles, CELL), jnp.int32),
             pltpu.VMEM((n, tiles, CELL, LAT), BF),
@@ -319,9 +341,16 @@
     own, second = pl.pallas_call(
         tile_kernel,
         out_shape=[jax.ShapeDtypeStruct(positions.shape, F32), jax.ShapeDtypeStruct((tiles, 3, CELL), F32)],
-        in_specs=[smem] * 4 + [vmem, anywhere, anywhere] + [vmem] * 6,
+        in_specs=[smem] * 4 + [anywhere] * 9,
         out_specs=[vmem] * 2,
         scratch_shapes=[
+            pltpu.VMEM(positions.shape, BF),
+            pltpu.VMEM((n, *positions.shape), BF),
+            pltpu.VMEM(w_first.shape, BF),
+            pltpu.VMEM(w_second.shape, BF),
+            pltpu.VMEM(radial_weight.shape, BF),
+            pltpu.VMEM(mix_weight.shape, BF),
+            pltpu.VMEM((1, LAT), F32),
             pltpu.VMEM((tiles, CELL, LAT), BF),
             pltpu.VMEM((tiles, CELL, LAT), BF),
             pltpu.VMEM((tiles, 3, CELL), F32),
@@ -339,8 +368,9 @@
             pltpu.VMEM((3, NB, W), F32),
             dma((tiles,)),
             dma((tiles,)),
+            dma((7,)),
         ],
-        compiler_params=pltpu.CompilerParams(vmem_limit_bytes=40 << 20),
+        compiler_params=pltpu.CompilerParams(vmem_limit_bytes=60 << 20),
         name="tiles",
     )(
         tile_first, tile_second, count_first, count_second, positions, features, got, got_pos, w_first, w_second,

time: 82.2 us -> 83.1 us (1.011)
  the two profiles are of different devices: /device:TPU:35 before, /device:TPU:0 now
where the time goes in v3:
time: 83.1 us; the launch traced here: 82.4 us
  Pallas kernels  80.8 us (97%)
  local copies, waits for them, and re-layouts  1.48 us (2%)
    pallas_call x1, Pallas kernels, on_device(): pl.pallas_call(tile_kernel, out_shape=[jax.ShapeDtypeStruct(positions.sha...  40.8 us
    pallas_call x1, Pallas kernels, on_device(): pl.pallas_call(functools.partial(fetch_kernel, tiles), out_shape=[jax.Sha...  25.3 us
    pallas_call x1, Pallas kernels, on_device(): pl.pallas_call(functools.partial(return_kernel, tiles), out_shape=jax.Sha...  14.8 us

profile of v3, /device:TPU:0, one launch (start us, length us, event | category | flops | bytes accessed | tf_op | source)
XLA Modules:
  0.0 82.4 jit_solution(6742137511246988839)
XLA Ops:
  0.0 25.3 %fetch.1 = (s32[3,8,128]{2,1,0:T(8,128)}, bf16[3,8,128,128]{3,2,1,0:T(8,128)(2,1)}, bf16[3,3,4096]{2,1,0:T(4,128)(2,1)}) custom-call(s32[8]{0:T(128)} %ts_ref.3, bf16[3,4096]{1,0:T(4,128)(2,1)} %pos_any.1, bf16[32,128,128]{2,1,0:T(8,128)(2,1)} %bitcast.2), custom_call_target="tpu_custom_call" | custom-call | tf_op jit(solution)/shard_map/fetch/pallas_call | solution.py:320
  25.3 40.8 %tiles.1 = (f32[3,4096]{1,0:T(4,128)}, f32[8,3,128]{2,1,0:T(4,128)}) custom-call(s32[8]{0:T(128)} %tf_ref.1, s32[8]{0:T(128)} %ts_ref.3, s32[8]{0:T(128)} %ca_ref.1, s32[8]{0:T(128)} %cb_ref.1, bf16[3,4096]{1,0:T(4,128)(2,1)} %pos_any.1, bf16[4096,128]{1,0:T(8,128)(2,1)} %feat_ref.1, bf16[3,8,128,128]{3,2,1,0:T(8,128)(2,1)} %get-tuple-element.11.got_ref, ...), custom_call_target="tpu_custom_call" | custom-call | tf_op jit(solution)/shard_map/tiles/pallas_call | solution.py:341
  66.1 14.8 %return.1 = f32[3,4096]{1,0:T(4,128)} custom-call(s32[3,8,128]{2,1,0:T(8,128)} %get-tuple-element.10.ask_ref, f32[3,4096]{1,0:T(4,128)} %get-tuple-element.13.own_ref, f32[8,3,128]{2,1,0:T(4,128)} %get-tuple-element.14.second_ref), custom_call_target="tpu_custom_call" | custom-call | tf_op jit(solution)/shard_map/return/pallas_call | solution.py:379
  80.9 1.5 %copy.13 = f32[3,4096]{1,0:T(4,128)} copy(f32[3,4096]{1,0:T(4,128)} %return.1) | data formatting | bytes 98304

commit v4 on v3

--- a/solution.py
+++ b/solution.py
@@ -14,6 +14,7 @@
 ROWS = 16
 SUB = 8
 PIECE = 2
+GROUPS = 4
 WAYS = ((0, 1), (1, 0), (1, 1))
 MESH = pl.DeviceIdType.MESH
 SPREAD = 2.8853900817779268**0.5
@@ -38,9 +39,18 @@
     return lax.rem(g + n_grp, n_grp), lax.rem(d + n_dev, n_dev)
 
 
+def remote(src, dst, send, recv, to):
+    copy = pltpu.make_async_remote_copy(
+        src_ref=src, dst_ref=dst, send_sem=send, recv_sem=recv, device_id=to, device_id_type=MESH
+    )
+    copy.start()
+    return copy
+
+
 def fetch_kernel(
-    n_tiles, ts_ref, pos_ref, feat_any, ask_ref, got_ref, gotpos_ref,
-    feat_ref, feat_sem, mine, numbers, out_ref, ask_send, ask_recv, local_sem, feat_send, feat_recv, pos_send, pos_recv,
+    n_tiles, tf_ref, ts_ref, pos_any, feat_any, ask_ref, fa_ref, fb_ref, gotpos_ref,
+    feat_ref, feat_sem, mine, numbers, corner_out, corner_in, side_out, side_in, up_out, up_in,
+    ask_send, ask_recv, local_sem, corner_send, corner_recv, up_send, up_recv, side_send, side_recv, pos_send, pos_recv,
 ):
     features = pltpu.make_async_copy(feat_any, feat_ref, feat_sem)
     features.start()
@@ -52,75 +62,76 @@
         mine[t : t + 1, :] = jnp.full((1, CELL), ts_ref[t], jnp.int32)
     pl.semaphore_wait(barrier, 2 * len(WAYS))
 
-    asks = []
-    for w, (g, d) in enumerate(WAYS):
-        copy = pltpu.make_async_remote_copy(
-            src_ref=mine, dst_ref=ask_ref.at[w], send_sem=ask_send.at[w], recv_sem=ask_recv.at[w],
-            device_id=other(-g, -d), device_id_type=MESH,
-        )
-        copy.start()
-        asks.append(copy)
-    sent = []
-    for w, (g, d) in enumerate(WAYS):
-        copy = pltpu.make_async_remote_copy(
-            src_ref=pos_ref, dst_ref=gotpos_ref.at[w], send_sem=pos_send.at[w], recv_sem=pos_recv.at[w],
-            device_id=other(g, d), device_id_type=MESH,
-        )
-        copy.start()
-        sent.append(copy)
+    asks = [
+        remote(mine, ask_ref.at[w], ask_send.at[w], ask_recv.at[w], other(-g, -d)) for w, (g, d) in enumerate(WAYS)
+    ]
+    sent = [
+        remote(pos_any, gotpos_ref.at[w], pos_send.at[w], pos_recv.at[w], other(g, d)) for w, (g, d) in enumerate(WAYS)
+    ]
     features.wait()
-    for w in (2, 1, 0):
+
+    def hear(w):
         asks[w].wait_recv()
         local = pltpu.make_async_copy(ask_ref.at[w], numbers.at[w], local_sem.at[w])
         local.start()
         local.wait()
-        for t in range(n_tiles):
-            out_ref[w, t] = feat_ref[lax.rem(numbers[w, t, 0], CELLS)]
-        copy = pltpu.make_async_remote_copy(
-            src_ref=out_ref.at[w], dst_ref=got_ref.at[w], send_sem=feat_send.at[w], recv_sem=feat_recv.at[w],
-            device_id=other(*WAYS[w]), device_id_type=MESH,
+
+    def pick(w, t):
+        return feat_ref[lax.rem(numbers[w, t, 0], CELLS)]
+
+    hear(2)
+    corners = []
+    for j in range(GROUPS):
+        part = range(j * n_tiles // GROUPS, (j + 1) * n_tiles // GROUPS)
+        for t in part:
+            corner_out[t] = pick(2, t)
+        at = pl.ds(part.start, len(part))
+        corners.append(
+            remote(corner_out.at[at], corner_in.at[at], corner_send.at[j], corner_recv.at[j], other(0, 1))
         )
-        copy.start()
-        sent.append(copy)
-    for copy in asks:
-        copy.wait_send()
+    hear(0)
+    for t in range(n_tiles):
+        side_out[t] = pick(0, t)
+    sides = remote(side_out, side_in, side_send, side_recv, other(0, 1))
+    hear(1)
+    for t in range(n_tiles):
+        up_out[t] = pick(1, t)
+    ups = []
+    for j in range(GROUPS):
+        part = range(j * n_tiles // GROUPS, (j + 1) * n_tiles // GROUPS)
+        corners[j].wait_recv()
+        for t in part:
+            near = ask_ref[1, t : t + 1, :] < 3 * CELLS
+            up_out[t] = jnp.where(near, up_out[t].astype(F32), corner_in[t].astype(F32)).astype(BF)
+        at = pl.ds(part.start, len(part))
+        ups.append(remote(up_out.at[at], up_in.at[at], up_send.at[j], up_recv.at[j], other(1, 0)))
+    for t in range(n_tiles):
+        fa_ref[t] = feat_ref[tf_ref[t]]
+        fb_ref[t] = feat_ref[lax.rem(ts_ref[t], CELLS)]
+    sides.wait_recv()
+    for t in range(n_tiles):
+        own = mine[t : t + 1, :] < CELLS
+        fb_ref[t] = jnp.where(own, fb_ref[t].astype(F32), side_in[t].astype(F32)).astype(BF)
+    for j in range(GROUPS):
+        ups[j].wait_recv()
+        for t in range(j * n_tiles // GROUPS, (j + 1) * n_tiles // GROUPS):
+            near = mine[t : t + 1, :] < 2 * CELLS
+            fb_ref[t] = jnp.where(near, fb_ref[t].astype(F32), up_in[t].astype(F32)).astype(BF)
     for copy in sent:
         copy.wait()
+    for copy in asks + corners + [sides] + ups:
+        copy.wait_send()
 
 
 def tile_kernel(
-    tf_ref, ts_ref, ca_ref, cb_ref, pos_any, feat_ref, got_ref, gotpos_any, wa_any, wb_any, wr_any, mix_any, ow_any,
+    tf_ref, ts_ref, ca_ref, cb_ref, pos_ref, gotpos_ref, fa_ref, fb_ref, wa_ref, wb_ref, wr_ref, mix_ref, ow_ref,
     own_ref, gb_ref,
-    pos_ref, gotpos_ref, wa_ref, wb_ref, wr_ref, mix_ref, ow_ref,
-    fa_ref, fb_ref, xb_ref, mixt_ref, owb_ref, lead, projc, d_ref, r2_ref, diff_ref, h_s, h2_s, y_s, slope_s, z_s,
-    sem_a, sem_b, sem_c,
+    xb_ref, mixt_ref, owb_ref, lead, projc, d_ref, r2_ref, diff_ref, h_s, h2_s, y_s, slope_s, z_s,
 ):
     W = ROWS * CELL
     PW = PIECE * CELL
     tiles = gb_ref.shape[0]
 
-    loads = []
-    for src, dst in (
-        (pos_any, pos_ref), (gotpos_any, gotpos_ref), (wa_any, wa_ref), (wb_any, wb_ref), (wr_any, wr_ref),
-        (mix_any, mix_ref), (ow_any, ow_ref),
-    ):
-        loads.append(pltpu.make_async_copy(src, dst, sem_c.at[len(loads)]))
-        loads[-1].start()
-    for t in range(tiles):
-        pltpu.make_async_copy(feat_ref.at[cell_slots(tf_ref[t])], fa_ref.at[t], sem_a.at[t]).start()
-        slots = cell_slots(lax.rem(ts_ref[t], CELLS))
-        source = ts_ref[t] // CELLS
-
-        @pl.when(source == 0)
-        def _():
-            pltpu.make_async_copy(feat_ref.at[slots], fb_ref.at[t], sem_b.at[t]).start()
-
-        @pl.when(source > 0)
-        def _():
-            pltpu.make_async_copy(got_ref.at[source - 1, t], fb_ref.at[t], sem_b.at[t]).start()
-
-    for load in loads:
-        load.wait()
     for t in range(tiles):
         slots = cell_slots(lax.rem(ts_ref[t], CELLS))
         source = ts_ref[t] // CELLS
@@ -129,9 +140,6 @@
     mixt_ref[...] = (mix_ref[...].astype(F32).T * 0.5).astype(BF)
     owb_ref[...] = jnp.broadcast_to(ow_ref[...], (CELL, LAT)).T
     own_ref[...] = jnp.zeros_like(own_ref)
-    for t in range(tiles):
-        pltpu.make_async_copy(feat_ref.at[pl.ds(0, CELL)], fa_ref.at[t], sem_a.at[t]).wait()
-        pltpu.make_async_copy(feat_ref.at[pl.ds(0, CELL)], fb_ref.at[t], sem_b.at[t]).wait()
 
     def prepare(t):
         swap = cb_ref[t] < ca_ref[t]
@@ -317,42 +325,38 @@
     anywhere = pl.BlockSpec(memory_space=pl.ANY)
     dma = pltpu.SemaphoreType.DMA
     n = len(WAYS)
-    ask, got, got_pos = pl.pallas_call(
+    cells = (tiles, CELL, LAT)
+    ask, first, second, got_pos = pl.pallas_call(
         functools.partial(fetch_kernel, tiles),
         out_shape=[
             jax.ShapeDtypeStruct((n, tiles, CELL), jnp.int32),
-            jax.ShapeDtypeStruct((n, tiles, CELL, LAT), BF),
+            jax.ShapeDtypeStruct(cells, BF),
+            jax.ShapeDtypeStruct(cells, BF),
             jax.ShapeDtypeStruct((n, *positions.shape), BF),
         ],
-        in_specs=[smem, anywhere, anywhere],
-        out_specs=[vmem, anywhere, anywhere],
+        in_specs=[smem, smem, anywhere, anywhere],
+        out_specs=[vmem, vmem, vmem, anywhere],
         scratch_shapes=[
             pltpu.VMEM((CELLS, CELL, LAT), BF),
             dma(()),
             pltpu.VMEM((tiles, CELL), jnp.int32),
             pltpu.SMEM((n, tiles, CELL), jnp.int32),
-            pltpu.VMEM((n, tiles, CELL, LAT), BF),
         ]
-        + [dma((n,))] * 7,
+        + [pltpu.VMEM(cells, BF)] * 6
+        + [dma((n,))] * 3
+        + [dma((GROUPS,))] * 4
+        + [dma(())] * 2
+        + [dma((n,))] * 2,
         compiler_params=pltpu.CompilerParams(collective_id=0, has_side_effects=True),
         name="fetch",
-    )(tile_second, positions, features.reshape(-1, CELL, LAT))
+    )(tile_first, tile_second, positions, features.reshape(-1, CELL, LAT))
     W = ROWS * CELL
-    own, second = pl.pallas_call(
+    own, partial = pl.pallas_call(
         tile_kernel,
         out_shape=[jax.ShapeDtypeStruct(positions.shape, F32), jax.ShapeDtypeStruct((tiles, 3, CELL), F32)],
-        in_specs=[smem] * 4 + [anywhere] * 9,
+        in_specs=[smem] * 4 + [vmem] * 9,
         out_specs=[vmem] * 2,
         scratch_shapes=[
-            pltpu.VMEM(positions.shape, BF),
-            pltpu.VMEM((n, *positions.shape), BF),
-            pltpu.VMEM(w_first.shape, BF),
-            pltpu.VMEM(w_second.shape, BF),
-            pltpu.VMEM(radial_weight.shape, BF),
-            pltpu.VMEM(mix_weight.shape, BF),
-            pltpu.VMEM((1, LAT), F32),
-            pltpu.VMEM((tiles, CELL, LAT), BF),
-            pltpu.VMEM((tiles, CELL, LAT), BF),
             pltpu.VMEM((tiles, 3, CELL), F32),
             pltpu.VMEM((LAT, LAT), BF),
             pltpu.VMEM((LAT, CELL), F32),
@@ -366,14 +370,11 @@
             pltpu.VMEM((LAT, W), F32),
             pltpu.VMEM((2, LAT, W), F32),
             pltpu.VMEM((3, NB, W), F32),
-            dma((tiles,)),
-            dma((tiles,)),
-            dma((7,)),
         ],
         compiler_params=pltpu.CompilerParams(vmem_limit_bytes=60 << 20),
         name="tiles",
     )(
-        tile_first, tile_second, count_first, count_second, positions, features, got, got_pos, w_first, w_second,
+        tile_first, tile_second, count_first, count_second, positions, got_pos, first, second, w_first, w_second,
         radial_weight, mix_weight, out_weight.reshape(1, LAT),
     )
     return pl.pallas_call(
@@ -384,7 +385,7 @@
         scratch_shapes=[pltpu.VMEM((n, tiles, 3, CELL), F32), dma((n,)), dma((n,))],
         compiler_params=pltpu.CompilerParams(collective_id=1, has_side_effects=True),
         name="return",
-    )(ask, own, second)
+    )(ask, own, partial)
 
 
 def solution(mesh):

time: 83.1 us -> 72.5 us (0.87)
  Pallas kernels: 80.8 us -> 70 us
    pallas_call x1, Pallas kernels: 14.8 us -> 8.28 us  [on_device(): pl.pallas_call(functools.partial(return_kernel, tiles), out_shape=jax.Sha...]
    pallas_call x1, Pallas kernels: 40.8 us -> 35.6 us  [on_device(): pl.pallas_call(tile_kernel, out_shape=[jax.ShapeDtypeStruct(positions.sha...]
where the time goes in v4:
time: 72.5 us; the launch traced here: 71.5 us
  Pallas kernels  70 us (97%)
  local copies, waits for them, and re-layouts  1.48 us (2%)
    pallas_call x1, Pallas kernels, on_device(): pl.pallas_call(tile_kernel, out_shape=[jax.ShapeDtypeStruct(positions.sha...  35.6 us
    pallas_call x1, Pallas kernels, on_device(): pl.pallas_call(functools.partial(fetch_kernel, tiles), out_shape=[jax.Sha...  26.1 us
    pallas_call x1, Pallas kernels, on_device(): pl.pallas_call(functools.partial(return_kernel, tiles), out_shape=jax.Sha...  8.28 us
    unnamed x1, local copies, waits for them, and re-layouts  1.48 us

profile of v4, /device:TPU:0, one launch (start us, length us, event | category | flops | bytes accessed | tf_op | source)
XLA Modules:
  0.0 71.5 jit_solution(5150371690722824242)
XLA Ops:
  0.0 26.1 %fetch.1 = (s32[3,8,128]{2,1,0:T(8,128)}, bf16[8,128,128]{2,1,0:T(8,128)(2,1)}, bf16[8,128,128]{2,1,0:T(8,128)(2,1)}, bf16[3,3,4096]{2,1,0:T(4,128)(2,1)}) custom-call(s32[8]{0:T(128)} %tf_ref.3, s32[8]{0:T(128)} %ts_ref.3, bf16[3,4096]{1,0:T(4,128)(2,1)} %pos_ref.1, bf16[32,128,128]{2,1,0:T(8,128)(2,1)} %bitcast.2), custom_call_target="tpu_custom_call" | custom-call | tf_op jit(solution)/shard_map/fetch/pallas_call | solution.py:329
  26.1 35.6 %tiles.1 = (f32[3,4096]{1,0:T(4,128)}, f32[8,3,128]{2,1,0:T(4,128)}) custom-call(s32[8]{0:T(128)} %tf_ref.3, s32[8]{0:T(128)} %ts_ref.3, s32[8]{0:T(128)} %ca_ref.1, s32[8]{0:T(128)} %cb_ref.1, bf16[3,4096]{1,0:T(4,128)(2,1)} %pos_ref.1, bf16[3,3,4096]{2,1,0:T(4,128)(2,1)} %get-tuple-element.12.gotpos_ref, bf16[8,128,128]{2,1,0:T(8,128)(2,1)} %get-tuple-element.13.fa_ref, ...), custom_call_target="tpu_custom_call" | custom-call | tf_op jit(solution)/shard_map/tiles/pallas_call | solution.py:354
  61.7 8.3 %return.1 = f32[3,4096]{1,0:T(4,128)} custom-call(s32[3,8,128]{2,1,0:T(8,128)} %get-tuple-element.11.ask_ref, f32[3,4096]{1,0:T(4,128)} %get-tuple-element.15.own_ref, f32[8,3,128]{2,1,0:T(4,128)} %get-tuple-element.16.second_ref), custom_call_target="tpu_custom_call" | custom-call | tf_op jit(solution)/shard_map/return/pallas_call | solution.py:380
  70.0 1.5 %copy.13 = f32[3,4096]{1,0:T(4,128)} copy(f32[3,4096]{1,0:T(4,128)} %return.1) | data formatting | bytes 98304

commit v5 on v4

--- a/solution.py
+++ b/solution.py
@@ -11,7 +11,7 @@
 CELLS = 32
 LAT = 128
 NB = 16
-ROWS = 16
+ROWS = 24
 SUB = 8
 PIECE = 2
 GROUPS = 4
@@ -302,16 +302,22 @@
     for copy in copies:
         copy.wait()
 
-    def one(c, _):
-        slots = cell_slots(c)
-        total = own_ref[:, slots]
-        for w in range(len(WAYS)):
-            for t in range(n_tiles):
-                total -= jnp.where(ask_ref[w, t : t + 1, :] == (w + 1) * CELLS + c, back_ref[w, t], 0.0)
-        out_ref[:, slots] = total
+    asked = [[ask_ref[w, t : t + 1, :] - (w + 1) * CELLS for t in range(n_tiles)] for w in range(len(WAYS))]
+
+    def four(u, _):
+        for i in range(4):
+            c = 4 * u + i
+            sums = []
+            for w in range(len(WAYS)):
+                hits = [jnp.where(asked[w][t] == c, back_ref[w, t], 0.0) for t in range(n_tiles)]
+                while len(hits) > 1:
+                    hits = [x + y for x, y in zip(hits[::2], hits[1::2], strict=True)]
+                sums += hits
+            slots = cell_slots(c)
+            out_ref[:, slots] = own_ref[:, slots] - (sums[0] + sums[1] + sums[2])
         return 0
 
-    lax.fori_loop(0, CELLS, one, 0)
+    lax.fori_loop(0, CELLS // 4, four, 0)
 
 
 def on_device(

time: 72.5 us -> 74.2 us (1.023)
  Pallas kernels: 70 us -> 72.3 us
    pallas_call x1, Pallas kernels: 35.6 us -> 40.3 us  [on_device(): pl.pallas_call(tile_kernel, out_shape=[jax.ShapeDtypeStruct(positions.sha...]
    pallas_call x1, Pallas kernels: 8.28 us -> 5.94 us  [on_device(): pl.pallas_call(functools.partial(return_kernel, tiles), out_shape=jax.Sha...]
where the time goes in v5:
time: 74.2 us; the launch traced here: 73.8 us
  Pallas kernels  72.3 us (97%)
  local copies, waits for them, and re-layouts  1.48 us (2%)
    pallas_call x1, Pallas kernels, on_device(): pl.pallas_call(tile_kernel, out_shape=[jax.ShapeDtypeStruct(positions.sha...  40.3 us
    pallas_call x1, Pallas kernels, on_device(): pl.pallas_call(functools.partial(fetch_kernel, tiles), out_shape=[jax.Sha...  26.1 us
    pallas_call x1, Pallas kernels, on_device(): pl.pallas_call(functools.partial(return_kernel, tiles), out_shape=jax.Sha...  5.94 us

profile of v5, /device:TPU:0, one launch (start us, length us, event | category | flops | bytes accessed | tf_op | source)
XLA Modules:
  0.0 73.8 jit_solution(2737771533652617173)
XLA Ops:
  0.0 26.1 %fetch.1 = (s32[3,8,128]{2,1,0:T(8,128)}, bf16[8,128,128]{2,1,0:T(8,128)(2,1)}, bf16[8,128,128]{2,1,0:T(8,128)(2,1)}, bf16[3,3,4096]{2,1,0:T(4,128)(2,1)}) custom-call(s32[8]{0:T(128)} %tf_ref.3, s32[8]{0:T(128)} %ts_ref.3, bf16[3,4096]{1,0:T(4,128)(2,1)} %pos_ref.1, bf16[32,128,128]{2,1,0:T(8,128)(2,1)} %bitcast.2), custom_call_target="tpu_custom_call" | custom-call | tf_op jit(solution)/shard_map/fetch/pallas_call | solution.py:335
  26.1 40.3 %tiles.1 = (f32[3,4096]{1,0:T(4,128)}, f32[8,3,128]{2,1,0:T(4,128)}) custom-call(s32[8]{0:T(128)} %tf_ref.3, s32[8]{0:T(128)} %ts_ref.3, s32[8]{0:T(128)} %ca_ref.1, s32[8]{0:T(128)} %cb_ref.1, bf16[3,4096]{1,0:T(4,128)(2,1)} %pos_ref.1, bf16[3,3,4096]{2,1,0:T(4,128)(2,1)} %get-tuple-element.12.gotpos_ref, bf16[8,128,128]{2,1,0:T(8,128)(2,1)} %get-tuple-element.13.fa_ref, ...), custom_call_target="tpu_custom_call" | custom-call | tf_op jit(solution)/shard_map/tiles/pallas_call | solution.py:360
  66.4 5.9 %return.1 = f32[3,4096]{1,0:T(4,128)} custom-call(s32[3,8,128]{2,1,0:T(8,128)} %get-tuple-element.11.ask_ref, f32[3,4096]{1,0:T(4,128)} %get-tuple-element.15.own_ref, f32[8,3,128]{2,1,0:T(4,128)} %get-tuple-element.16.second_ref), custom_call_target="tpu_custom_call" | custom-call | tf_op jit(solution)/shard_map/return/pallas_call | solution.py:386
  72.3 1.5 %copy.13 = f32[3,4096]{1,0:T(4,128)} copy(f32[3,4096]{1,0:T(4,128)} %return.1) | data formatting | bytes 98304

commit v6 on v5

--- a/solution.py
+++ b/solution.py
@@ -62,9 +62,10 @@
         mine[t : t + 1, :] = jnp.full((1, CELL), ts_ref[t], jnp.int32)
     pl.semaphore_wait(barrier, 2 * len(WAYS))
 
-    asks = [
-        remote(mine, ask_ref.at[w], ask_send.at[w], ask_recv.at[w], other(-g, -d)) for w, (g, d) in enumerate(WAYS)
-    ]
+    asks = {}
+    for w in (2, 0, 1):
+        g, d = WAYS[w]
+        asks[w] = remote(mine, ask_ref.at[w], ask_send.at[w], ask_recv.at[w], other(-g, -d))
     sent = [
         remote(pos_any, gotpos_ref.at[w], pos_send.at[w], pos_recv.at[w], other(g, d)) for w, (g, d) in enumerate(WAYS)
     ]
@@ -119,7 +120,7 @@
             fb_ref[t] = jnp.where(near, fb_ref[t].astype(F32), up_in[t].astype(F32)).astype(BF)
     for copy in sent:
         copy.wait()
-    for copy in asks + corners + [sides] + ups:
+    for copy in list(asks.values()) + corners + [sides] + ups:
         copy.wait_send()
 
 
@@ -162,12 +163,12 @@
             r2 = r2 + d * d
         r2_ref[t] = r2 * SPREAD
 
-    def prepare_two(u, _):
-        prepare(2 * u)
-        prepare(2 * u + 1)
+    def prepare_four(u, _):
+        for i in range(4):
+            prepare(4 * u + i)
         return 0
 
-    lax.fori_loop(0, tiles // 2, prepare_two, 0)
+    lax.fori_loop(0, tiles // 4, prepare_four, 0)
 
     hot = lax.broadcasted_iota(jnp.int32, (16, SUB * CELL), 0)
     hot = hot == lax.broadcasted_iota(jnp.int32, (16, SUB * CELL), 1) // CELL
@@ -276,20 +277,27 @@
         def _():
             own_ref[:, cell_slots(lax.rem(ts_ref[t], CELLS))] -= gb
 
-    def finish_two(u, _):
-        one = finish(2 * u)
-        two = finish(2 * u + 1)
-        put(2 * u, *one)
-        put(2 * u + 1, *two)
+    def finish_four(u, _):
+        found = [finish(4 * u + i) for i in range(4)]
+        for i in range(4):
+            put(4 * u + i, *found[i])
         return 0
 
-    lax.fori_loop(0, tiles // 2, finish_two, 0)
-
-
-def return_kernel(n_tiles, ask_ref, own_ref, second_ref, out_ref, back_ref, send_sem, recv_sem):
+    lax.fori_loop(0, tiles // 4, finish_four, 0)
+
+
+def return_kernel(
+    n_tiles, ask_any, own_any, second_ref, out_ref, ask_ref, own_ref, back_ref, load_sem, send_sem, recv_sem
+):
     barrier = pltpu.get_barrier_semaphore()
     for g, d in WAYS:
         pl.semaphore_signal(barrier, inc=1, device_id=other(g, d), device_id_type=MESH)
+    loads = [
+        pltpu.make_async_copy(ask_any, ask_ref, load_sem.at[0]),
+        pltpu.make_async_copy(own_any, own_ref, load_sem.at[1]),
+    ]
+    for load in loads:
+        load.start()
     pl.semaphore_wait(barrier, len(WAYS))
     copies = []
     for w, (g, d) in enumerate(WAYS):
@@ -299,7 +307,7 @@
         )
         copy.start()
         copies.append(copy)
-    for copy in copies:
+    for copy in loads + copies:
         copy.wait()
 
     asked = [[ask_ref[w, t : t + 1, :] - (w + 1) * CELLS for t in range(n_tiles)] for w in range(len(WAYS))]
@@ -386,9 +394,16 @@
     return pl.pallas_call(
         functools.partial(return_kernel, tiles),
         out_shape=jax.ShapeDtypeStruct(positions.shape, F32),
-        in_specs=[vmem] * 3,
+        in_specs=[anywhere] * 3,
         out_specs=vmem,
-        scratch_shapes=[pltpu.VMEM((n, tiles, 3, CELL), F32), dma((n,)), dma((n,))],
+        scratch_shapes=[
+            pltpu.VMEM((n, tiles, CELL), jnp.int32),
+            pltpu.VMEM(positions.shape, F32),
+            pltpu.VMEM((n, tiles, 3, CELL), F32),
+            dma((2,)),
+            dma((n,)),
+            dma((n,)),
+        ],
         compiler_params=pltpu.CompilerParams(collective_id=1, has_side_effects=True),
         name="return",
     )(ask, own, partial)

time: 74.2 us -> 73.5 us (level)
  Pallas kernels: 72.3 us -> 71 us
    pallas_call x1, Pallas kernels: 40.3 us -> 37.2 us  [on_device(): pl.pallas_call(tile_kernel, out_shape=[jax.ShapeDtypeStruct(positions.sha...]
    pallas_call x1, Pallas kernels: 5.94 us -> 7.76 us  [on_device(): pl.pallas_call(functools.partial(return_kernel, tiles), out_shape=jax.Sha...]
where the time goes in v6:
time: 73.5 us; the launch traced here: 72.5 us
  Pallas kernels  71 us (97%)
  local copies, waits for them, and re-layouts  1.48 us (2%)
    pallas_call x1, Pallas kernels, on_device(): pl.pallas_call(tile_kernel, out_shape=[jax.ShapeDtypeStruct(positions.sha...  37.2 us
    pallas_call x1, Pallas kernels, on_device(): pl.pallas_call(functools.partial(fetch_kernel, tiles), out_shape=[jax.Sha...  26 us
    pallas_call x1, Pallas kernels, on_device(): pl.pallas_call(functools.partial(return_kernel, tiles), out_shape=jax.Sha...  7.76 us
    unnamed x1, local copies, waits for them, and re-layouts  1.48 us

profile of v6, /device:TPU:0, one launch (start us, length us, event | category | flops | bytes accessed | tf_op | source)
XLA Modules:
  0.0 72.5 jit_solution(14574001061146603812)
XLA Ops:
  0.0 26.0 %fetch.1 = (s32[3,8,128]{2,1,0:T(8,128)}, bf16[8,128,128]{2,1,0:T(8,128)(2,1)}, bf16[8,128,128]{2,1,0:T(8,128)(2,1)}, bf16[3,3,4096]{2,1,0:T(4,128)(2,1)}) custom-call(s32[8]{0:T(128)} %tf_ref.3, s32[8]{0:T(128)} %ts_ref.3, bf16[3,4096]{1,0:T(4,128)(2,1)} %pos_ref.1, bf16[32,128,128]{2,1,0:T(8,128)(2,1)} %bitcast.2), custom_call_target="tpu_custom_call" | custom-call | tf_op jit(solution)/shard_map/fetch/pallas_call | solution.py:343
  26.0 37.2 %tiles.1 = (f32[3,4096]{1,0:T(4,128)}, f32[8,3,128]{2,1,0:T(4,128)}) custom-call(s32[8]{0:T(128)} %tf_ref.3, s32[8]{0:T(128)} %ts_ref.3, s32[8]{0:T(128)} %ca_ref.1, s32[8]{0:T(128)} %cb_ref.1, bf16[3,4096]{1,0:T(4,128)(2,1)} %pos_ref.1, bf16[3,3,4096]{2,1,0:T(4,128)(2,1)} %get-tuple-element.12.gotpos_ref, bf16[8,128,128]{2,1,0:T(8,128)(2,1)} %get-tuple-element.13.fa_ref, ...), custom_call_target="tpu_custom_call" | custom-call | tf_op jit(solution)/shard_map/tiles/pallas_call | solution.py:368
  63.2 7.8 %return.1 = f32[3,4096]{1,0:T(4,128)} custom-call(s32[3,8,128]{2,1,0:T(8,128)} %get-tuple-element.11.ask_any, f32[3,4096]{1,0:T(4,128)} %get-tuple-element.15.own_any, f32[8,3,128]{2,1,0:T(4,128)} %get-tuple-element.16.second_ref), custom_call_target="tpu_custom_call" | custom-call | tf_op jit(solution)/shard_map/return/pallas_call | solution.py:394
  71.0 1.5 %copy.13 = f32[3,4096]{1,0:T(4,128)} copy(f32[3,4096]{1,0:T(4,128)} %return.1) | data formatting | bytes 98304

commit v7 on v6

--- a/solution.py
+++ b/solution.py
@@ -190,35 +190,37 @@
         return tuple(places)
 
     def step(it, carry):
-        at1, at2, at3, at4 = carry
+        before, now = carry
+        places = before + now
         rows = lambda c: pl.ds(pl.multiple_of(c * SUB, SUB), SUB)
-        slope_at = lax.rem(it, 2)
-        z_at = lax.rem(it, 3)
         owb = jnp.concatenate([owb_ref[...]] * PIECE, axis=1)
         for p in range(ROWS // PIECE):
-            cs = slice(p * PW, (p + 1) * PW)
+            cs, cs2, cs3, _ = (
+                slice(k * PW, (k + 1) * PW) for k in ((p - lag * per_sub) % (n_sub * per_sub) for lag in range(4))
+            )
             q = p % per_sub
             if q == 0:
-                (t1, c1), (t2, _), (t3, c3), (t4, c4) = (at[p // per_sub] for at in carry)
+                at = n_sub + p // per_sub
+                (t1, c1), (t2, _), (t3, c3), (t4, c4) = (places[at - lag] for lag in range(4))
                 in1 = jnp.minimum(t1, tiles - 1)
                 r2 = r2_ref[in1, rows(c1), :]
                 lhs = jnp.concatenate([wr_ref[...] * jnp.asarray(0.5, BF), lead[in1, c1]], axis=0)
                 pc = jnp.concatenate([projc[jnp.minimum(t2, tiles - 1)]] * PIECE, axis=1)
                 cores = []
                 readouts = []
-            ds = (y_s[:, cs] * slope_s[slope_at, :, cs]).astype(BF)
-            z = z_s[z_at, :, cs]
-            h2 = h2_s[:, cs]
+            ds = (y_s[:, cs] * slope_s[:, cs]).astype(BF)
+            z = z_s[:, cs]
+            h2 = h2_s[:, cs3]
             tt = jnp.tanh(h2)
             v = owb * (1 + tt)
             act = h2 * v
             ro = jnp.sum(act, axis=0, keepdims=True)
             back = (v + act * (1 - tt)).astype(BF)
-            h = h_s[:, cs] + pc
+            h = h_s[:, cs2] + pc
             tt = jnp.tanh(h)
             v = 1 + tt
             act = h * v
-            slope_s[slope_at, :, cs] = v + act * (1 - tt)
+            slope_s[:, cs2] = v + act * (1 - tt)
             latent = act.astype(BF)
             gs = []
             zs = []
@@ -227,19 +229,19 @@
                 g = jnp.exp2(-(o * o))
                 gs.append(g.astype(BF))
                 zs.append(g * o)
-            z_s[z_at, :, cs] = jnp.concatenate(zs, axis=1)
+            z_s[:, cs] = jnp.concatenate(zs, axis=1)
             rhs = jnp.concatenate([jnp.concatenate(gs, axis=1), hot[:, q * PW : (q + 1) * PW]], axis=0)
-            y_s[:, cs] = dot(mix_ref[...], back, ((1,), (0,)))
+            y_s[:, cs3] = dot(mix_ref[...], back, ((1,), (0,)))
             h_s[:, cs] = dot(lhs, rhs, ((0,), (0,)))
             z = dot(wr_ref[...], ds, ((1,), (0,))) * z
-            h2_s[:, cs] = dot(mixt_ref[...], latent, ((1,), (0,)))
+            h2_s[:, cs2] = dot(mixt_ref[...], latent, ((1,), (0,)))
             for i in range(PIECE):
                 cores.append(jnp.sum(z[:, i * CELL : (i + 1) * CELL], axis=0, keepdims=True))
                 readouts.append(ro[:, i * CELL : (i + 1) * CELL])
             if q == per_sub - 1:
                 d_ref[0, t4, rows(c4), :] = jnp.concatenate(cores, axis=0)
                 d_ref[1, t3, rows(c3), :] = jnp.concatenate(readouts, axis=0)
-        return following(at1[-1]), at1, at2, at3
+        return now, following(now[-1])
 
     total = jnp.int32(0)
     for t in range(tiles):
@@ -248,7 +250,7 @@
     start = (zero, zero)
     start = ((start,) + following(start))[:n_sub]
     idle = ((jnp.int32(tiles), zero),) * n_sub
-    lax.fori_loop(0, (total + n_sub - 1) // n_sub + 3, step, (start, idle, idle, idle))
+    lax.fori_loop(0, (total + n_sub + 2) // n_sub, step, (idle, start))
 
     def finish(t):
         ca, cb = ca_ref[t], cb_ref[t]
@@ -382,8 +384,8 @@
             pltpu.VMEM((LAT, W), F32),
             pltpu.VMEM((LAT, W), F32),
             pltpu.VMEM((LAT, W), F32),
-            pltpu.VMEM((2, LAT, W), F32),
-            pltpu.VMEM((3, NB, W), F32),
+            pltpu.VMEM((LAT, W), F32),
+            pltpu.VMEM((NB, W), F32),
         ],
         compiler_params=pltpu.CompilerParams(vmem_limit_bytes=60 << 20),
         name="tiles",

time: 73.5 us -> 69.6 us (0.947)
  the two profiles are of different devices: /device:TPU:0 before, /device:TPU:2 now
where the time goes in v7:
time: 69.6 us; the launch traced here: 68.4 us
  Pallas kernels  66.9 us (96%)
  local copies, waits for them, and re-layouts  1.48 us (2%)
    pallas_call x1, Pallas kernels, on_device(): pl.pallas_call(tile_kernel, out_shape=[jax.ShapeDtypeStruct(positions.sha...  32 us
    pallas_call x1, Pallas kernels, on_device(): pl.pallas_call(functools.partial(fetch_kernel, tiles), out_shape=[jax.Sha...  22.6 us
    pallas_call x1, Pallas kernels, on_device(): pl.pallas_call(functools.partial(return_kernel, tiles), out_shape=jax.Sha...  12.3 us
    unnamed x1, local copies, waits for them, and re-layouts  1.48 us

profile of v7, /device:TPU:2, one launch (start us, length us, event | category | flops | bytes accessed | tf_op | source)
XLA Modules:
  0.0 68.4 jit_solution(18035431418473518807)
XLA Ops:
  0.0 22.6 %fetch.1 = (s32[3,8,128]{2,1,0:T(8,128)}, bf16[8,128,128]{2,1,0:T(8,128)(2,1)}, bf16[8,128,128]{2,1,0:T(8,128)(2,1)}, bf16[3,3,4096]{2,1,0:T(4,128)(2,1)}) custom-call(s32[8]{0:T(128)} %tf_ref.3, s32[8]{0:T(128)} %ts_ref.3, bf16[3,4096]{1,0:T(4,128)(2,1)} %pos_ref.1, bf16[32,128,128]{2,1,0:T(8,128)(2,1)} %bitcast.2), custom_call_target="tpu_custom_call" | custom-call | tf_op jit(solution)/shard_map/fetch/pallas_call | solution.py:345
  22.7 32.0 %tiles.1 = (f32[3,4096]{1,0:T(4,128)}, f32[8,3,128]{2,1,0:T(4,128)}) custom-call(s32[8]{0:T(128)} %tf_ref.3, s32[8]{0:T(128)} %ts_ref.3, s32[8]{0:T(128)} %ca_ref.1, s32[8]{0:T(128)} %cb_ref.1, bf16[3,4096]{1,0:T(4,128)(2,1)} %pos_ref.1, bf16[3,3,4096]{2,1,0:T(4,128)(2,1)} %get-tuple-element.12.gotpos_ref, bf16[8,128,128]{2,1,0:T(8,128)(2,1)} %get-tuple-element.13.fa_ref, ...), custom_call_target="tpu_custom_call" | custom-call | tf_op jit(solution)/shard_map/tiles/pallas_call | solution.py:370
  54.7 12.3 %return.1 = f32[3,4096]{1,0:T(4,128)} custom-call(s32[3,8,128]{2,1,0:T(8,128)} %get-tuple-element.11.ask_any, f32[3,4096]{1,0:T(4,128)} %get-tuple-element.15.own_any, f32[8,3,128]{2,1,0:T(4,128)} %get-tuple-element.16.second_ref), custom_call_target="tpu_custom_call" | custom-call | tf_op jit(solution)/shard_map/return/pallas_call | solution.py:396
  66.9 1.5 %copy.13 = f32[3,4096]{1,0:T(4,128)} copy(f32[3,4096]{1,0:T(4,128)} %return.1) | data formatting | bytes 98304

commit v8 on v7

--- a/solution.py
+++ b/solution.py
@@ -11,7 +11,7 @@
 CELLS = 32
 LAT = 128
 NB = 16
-ROWS = 24
+ROWS = 32
 SUB = 8
 PIECE = 2
 GROUPS = 4
@@ -195,7 +195,7 @@
         rows = lambda c: pl.ds(pl.multiple_of(c * SUB, SUB), SUB)
         owb = jnp.concatenate([owb_ref[...]] * PIECE, axis=1)
         for p in range(ROWS // PIECE):
-            cs, cs2, cs3, _ = (
+            cs, cs2, cs3, cs4 = (
                 slice(k * PW, (k + 1) * PW) for k in ((p - lag * per_sub) % (n_sub * per_sub) for lag in range(4))
             )
             q = p % per_sub
@@ -208,8 +208,8 @@
                 pc = jnp.concatenate([projc[jnp.minimum(t2, tiles - 1)]] * PIECE, axis=1)
                 cores = []
                 readouts = []
-            ds = (y_s[:, cs] * slope_s[:, cs]).astype(BF)
-            z = z_s[:, cs]
+            ds = (y_s[:, cs4] * slope_s[:, cs4]).astype(BF)
+            z = z_s[:, cs4]
             h2 = h2_s[:, cs3]
             tt = jnp.tanh(h2)
             v = owb * (1 + tt)
@@ -231,10 +231,10 @@
                 zs.append(g * o)
             z_s[:, cs] = jnp.concatenate(zs, axis=1)
             rhs = jnp.concatenate([jnp.concatenate(gs, axis=1), hot[:, q * PW : (q + 1) * PW]], axis=0)
+            h2_s[:, cs2] = dot(mixt_ref[...], latent, ((1,), (0,)))
+            z = dot(wr_ref[...], ds, ((1,), (0,))) * z
+            h_s[:, cs] = dot(lhs, rhs, ((0,), (0,)))
             y_s[:, cs3] = dot(mix_ref[...], back, ((1,), (0,)))
-            h_s[:, cs] = dot(lhs, rhs, ((0,), (0,)))
-            z = dot(wr_ref[...], ds, ((1,), (0,))) * z
-            h2_s[:, cs2] = dot(mixt_ref[...], latent, ((1,), (0,)))
             for i in range(PIECE):
                 cores.append(jnp.sum(z[:, i * CELL : (i + 1) * CELL], axis=0, keepdims=True))
                 readouts.append(ro[:, i * CELL : (i + 1) * CELL])

time: 69.6 us -> 72.5 us (1.042)
  the two profiles are of different devices: /device:TPU:2 before, /device:TPU:0 now
where the time goes in v8:
time: 72.5 us; the launch traced here: 72.4 us
  Pallas kernels  70.9 us (98%)
  local copies, waits for them, and re-layouts  1.48 us (2%)
    pallas_call x1, Pallas kernels, on_device(): pl.pallas_call(tile_kernel, out_shape=[jax.ShapeDtypeStruct(positions.sha...  39.6 us
    pallas_call x1, Pallas kernels, on_device(): pl.pallas_call(functools.partial(fetch_kernel, tiles), out_shape=[jax.Sha...  26 us
    pallas_call x1, Pallas kernels, on_device(): pl.pallas_call(functools.partial(return_kernel, tiles), out_shape=jax.Sha...  5.29 us
    unnamed x1, local copies, waits for them, and re-layouts  1.48 us

profile of v8, /device:TPU:0, one launch (start us, length us, event | category | flops | bytes accessed | tf_op | source)
XLA Modules:
  0.0 72.4 jit_solution(11877827595139507407)
XLA Ops:
  0.0 26.0 %fetch.1 = (s32[3,8,128]{2,1,0:T(8,128)}, bf16[8,128,128]{2,1,0:T(8,128)(2,1)}, bf16[8,128,128]{2,1,0:T(8,128)(2,1)}, bf16[3,3,4096]{2,1,0:T(4,128)(2,1)}) custom-call(s32[8]{0:T(128)} %tf_ref.3, s32[8]{0:T(128)} %ts_ref.3, bf16[3,4096]{1,0:T(4,128)(2,1)} %pos_ref.1, bf16[32,128,128]{2,1,0:T(8,128)(2,1)} %bitcast.2), custom_call_target="tpu_custom_call" | custom-call | tf_op jit(solution)/shard_map/fetch/pallas_call | solution.py:345
  26.0 39.6 %tiles.1 = (f32[3,4096]{1,0:T(4,128)}, f32[8,3,128]{2,1,0:T(4,128)}) custom-call(s32[8]{0:T(128)} %tf_ref.3, s32[8]{0:T(128)} %ts_ref.3, s32[8]{0:T(128)} %ca_ref.1, s32[8]{0:T(128)} %cb_ref.1, bf16[3,4096]{1,0:T(4,128)(2,1)} %pos_ref.1, bf16[3,3,4096]{2,1,0:T(4,128)(2,1)} %get-tuple-element.12.gotpos_ref, bf16[8,128,128]{2,1,0:T(8,128)(2,1)} %get-tuple-element.13.fa_ref, ...), custom_call_target="tpu_custom_call" | custom-call | tf_op jit(solution)/shard_map/tiles/pallas_call | solution.py:370
  65.6 5.3 %return.1 = f32[3,4096]{1,0:T(4,128)} custom-call(s32[3,8,128]{2,1,0:T(8,128)} %get-tuple-element.11.ask_any, f32[3,4096]{1,0:T(4,128)} %get-tuple-element.15.own_any, f32[8,3,128]{2,1,0:T(4,128)} %get-tuple-element.16.second_ref), custom_call_target="tpu_custom_call" | custom-call | tf_op jit(solution)/shard_map/return/pallas_call | solution.py:396
  70.9 1.5 %copy.13 = f32[3,4096]{1,0:T(4,128)} copy(f32[3,4096]{1,0:T(4,128)} %return.1) | data formatting | bytes 98304
